TPU v7x, 128 devices: a whole 4x4x4 slice. The times are simulated.
128 devices in a mesh: dp: 4 (over x_hi, core), tm: 32 (over z, y, x_lo).
Axes of the slice: x: 4 (x_hi: 2, x_lo: 2; x = x_hi * 2 + x_lo), y: 4, z: 4, core: 2. Of those that a mesh axis runs over, the one named last changes fastest.
Arguments:
- features: bfloat16 [8, 256, 81, 1152], P('dp', 'tm'), may hold values from -6 to 6
- shot_ids: int32 [8, 256], P('dp'), may hold values from 0 to 15, never falling along the last dimension, each value on 1 to 48 neighbouring positions
- band_width: int32 [8, 4], P('dp'), may hold values from 2 to 64, as said below
- proj_weight: bfloat16 [1152, 3584], replicated, may hold values from -0.1875 to 0.1875
- cotangent: bfloat16 [8, 32, 81, 3584], P('dp', 'tm'), may hold values from -1.5 to 1.5
Outputs:
- projected: bfloat16 [8, 32, 81, 3584], P('dp', 'tm')
- weight_grad: float32 [1152, 3584], P(('dp', 'tm'))
Inputs may be any that keep to these rules, and one draw needn't show every extreme that they name: `shot_ids`: shot numbers never fall along a video; each shot has 1 to 48 frames. `band_width`: one block of each video has 64.
All inputs are finite; a program needn't handle non-finite values.
Results may differ from a plain program's by a relative error of at most 0.019.
Values may be sent and summed in bfloat16 or wider, within the bound.
A program may use at most 192 MiB of HBM per device.

v0:
```python
import jax
import jax.numpy as jnp
from jax import lax
from jax.sharding import PartitionSpec as P

BLOCK = 64
POOL = 8


decay_length = 16.0


def gelu_tanh(values):
    return jax.nn.gelu(values, approximate=True)


def mixing_weights(shot_ids, band_width):
    block_shots = shot_ids.reshape(shot_ids.shape[:-1] + (-1, BLOCK))
    position = jnp.arange(BLOCK)
    distance = jnp.abs(position[:, None] - position[None, :])
    same_shot = block_shots[..., :, None] == block_shots[..., None, :]
    allowed = same_shot & (distance <= band_width[..., None, None])
    raw_weight = jnp.where(
        allowed, jnp.exp(-distance.astype(jnp.float32) / decay_length), jnp.float32(0.0)
    )
    return (raw_weight / jnp.sum(raw_weight, axis=-1, keepdims=True)).astype(jnp.bfloat16)


def combine_weights(mix_weight):
    lead = mix_weight.shape[:-2]
    grouped = mix_weight.astype(jnp.float32).reshape(lead + (BLOCK // POOL, POOL, BLOCK))
    return (grouped.sum(axis=-2) * 0.125).astype(jnp.bfloat16)


def per_device(features, shot_ids, band_width, proj_weight, cotangent):
    count_videos, frames_dev, tokens_frame, feature_width = features.shape
    total_frames = shot_ids.shape[1]
    count_blocks = total_frames // BLOCK
    flattened = features.reshape(count_videos, frames_dev, tokens_frame * feature_width)
    combined = combine_weights(mixing_weights(shot_ids, band_width))
    spread = lax.all_to_all(flattened, "tm", split_axis=2, concat_axis=1, tiled=True)
    share_width = spread.shape[2]
    blocks = spread.reshape(count_videos, count_blocks, BLOCK, share_width)
    pooled_share = jnp.einsum(
        "vbps,vbsf->vbpf", combined, blocks, preferred_element_type=jnp.float32
    )
    pooled_share = pooled_share.astype(jnp.bfloat16).reshape(
        count_videos, total_frames // POOL, share_width
    )
    pooled = lax.all_to_all(pooled_share, "tm", split_axis=1, concat_axis=2, tiled=True)
    pooled_rows = pooled.reshape(-1, feature_width)
    preact = jnp.dot(pooled_rows, proj_weight, preferred_element_type=jnp.float32)
    activation, pullback = jax.vjp(gelu_tanh, preact)
    hidden_width = proj_weight.shape[1]
    grad_preact = pullback(cotangent.reshape(-1, hidden_width).astype(jnp.float32))[0].astype(
        jnp.bfloat16
    )
    grad_term = jnp.einsum(
        "rd,rh->dh", pooled_rows, grad_preact, preferred_element_type=jnp.float32
    )
    weight_grad = lax.psum_scatter(grad_term, ("dp", "tm"), scatter_dimension=0, tiled=True)
    projected = activation.astype(jnp.bfloat16).reshape(cotangent.shape)
    return (projected, weight_grad)


def solution(mesh):
    return jax.shard_map(
        per_device,
        mesh=mesh,
        in_specs=(
            P("dp", "tm", None, None),
            P("dp", None),
            P("dp", None),
            P(),
            P("dp", "tm", None, None),
        ),
        out_specs=(P("dp", "tm", None, None), P(("dp", "tm"), None)),
        check_vma=False,
    )
```

profile of v0, /device:TPU:0, one launch (start us, length us, event | category | flops | bytes accessed | tf_op | source)
XLA Modules:
  0.0 586.5 jit_solution(2503123138310756598)
XLA Ops:
  7.2 86.8 %copy.25 = bf16[2,8,81,1152]{1,0,3,2:T(2,128)(2,1)} copy(bf16[2,8,81,1152]{3,1,2,0:T(8,128)(2,1)} %param.5) | data formatting | bytes 5971968 | tf_op args[0]
  93.9 54.2 %reshape.70 = bf16[32,2,23328]{2,1,0:T(2,128)(2,1)} reshape(bf16[93312,2,8]{2,1,0:T(2,128)(2,1)} %bitcast.17) | data formatting | bytes 5971968
  148.1 9.5 %all-to-all-start = ((bf16[32,2,23328]{2,1,0:T(2,128)(2,1)}), bf16[32,2,23328]{2,1,0:T(2,128)(2,1)S(1)}, u32[]{:S(2)}, u32[]{:S(2)}) async-start(bf16[32,2,23328]{2,1,0:T(2,128)(2,1)} %reshape.70), calls=%async_computation | async-start | bytes 5996544 | tf_op jit(solution)/shard_map/all_to_all | solution.py:41
  157.7 0.1 eq.24
  157.9 0.3 select_reduce_fusion
  158.2 0.1 multiply_exponential_fusion.1
  158.4 0.2 convert_reduce_fusion
  158.6 39.3 %all-to-all-done = bf16[32,2,23328]{2,1,0:T(2,128)(2,1)S(1)} async-done(((bf16[32,2,23328]{2,1,0:T(2,128)(2,1)}), bf16[32,2,23328]{2,1,0:T(2,128)(2,1)S(1)}, u32[]{:S(2)}, u32[]{:S(2)}) %all-to-all-start) | async-done | bytes 2986016 | tf_op jit(solution)/shard_map/all_to_all | solution.py:41
  198.0 41.0 %reshape.71 = bf16[93312,2,8]{2,1,0:T(2,128)(2,1)} reshape(bf16[32,2,23328]{2,1,0:T(2,128)(2,1)S(1)} %all-to-all-done) | data formatting | bytes 5971968
  239.0 92.6 %copy.33 = bf16[2,8,32,2916]{3,1,2,0:T(8,128)(2,1)S(1)} copy(bf16[2,8,32,2916]{1,0,3,2:T(2,128)(2,1)} %bitcast.16) | data formatting | bytes 5971968 | tf_op jit(solution)/shard_map/all_to_all | solution.py:41
  331.5 0.5 fusion
  332.0 1.1 copy.28
  333.1 6.0 %all-to-all-start.1 = ((bf16[2,32,2916]{2,0,1:T(2,128)(2,1)}), bf16[2,32,2916]{2,0,1:T(2,128)(2,1)S(1)}, u32[]{:S(2)}, u32[]{:S(2)}) async-start(bf16[2,32,2916]{2,0,1:T(2,128)(2,1)} %copy.28), calls=%async_computation.1 | async-start | bytes 753664 | tf_op jit(solution)/shard_map/all_to_all | solution.py:50
  339.1 0.2 all-reduce.3.cloned.1.call-start
  339.3 1.5 copy.30
  340.9 1.7 reshape.69
  342.6 6.6 %all-to-all-done.1 = bf16[2,32,2916]{2,0,1:T(2,128)(2,1)S(1)} async-done(((bf16[2,32,2916]{2,0,1:T(2,128)(2,1)}), bf16[2,32,2916]{2,0,1:T(2,128)(2,1)S(1)}, u32[]{:S(2)}, u32[]{:S(2)}) %all-to-all-start.1) | async-done | bytes 373280 | tf_op jit(solution)/shard_map/all_to_all | solution.py:50
  349.2 0.9 reshape.67
  350.1 5.3 multiply_convert_fusion
  355.5 8.3 %fusion.8 = f32[1152,3584]{1,0:T(8,128)} fusion(bf16[162,1152]{1,0:T(8,128)(2,1)S(1)} %reshape.67, f32[162,3584]{1,0:T(8,128)S(1)} %get-tuple-element.13, f32[162,3584]{1,0:T(8,128)S(1)} %copy-done), kind=kOutput, calls=%fused_computation.12 | convolution fusion | flops 1349332992 | bytes 21533184 | tf_op jit(solution)/shard_map/rd,rh->dh/dot_general | solution.py:58
  363.8 0.2 reshape.68
  364.0 1.9 copy.31
  365.9 212.0 %all-reduce.3.cloned.1.call-done = f32[1152,3584]{1,0:T(8,128)} async-done(((f32[1152,3584]{1,0:T(8,128)}), f32[1152,3584]{1,0:T(8,128)}) %all-reduce.3.cloned.1.call-update) | async-done | bytes 16515088
  577.9 1.7 constant_dynamic-slice_fusion
  (14 shorter events, 0.3 us)
Async XLA Ops:
  148.1 9.5 %copy-start.1 = (s32[2,256]{1,0:T(2,128)S(1)}, s32[2,256]{1,0:T(2,128)}, u32[]{:S(2)}) copy-start(s32[2,256]{1,0:T(2,128)} %param.6) | copy-start | bytes 6148
  148.1 9.7 %copy-start.2 = (s32[2,4]{1,0:T(2,128)S(1)}, s32[2,4]{1,0:T(2,128)}, u32[]{:S(2)}) copy-start(s32[2,4]{1,0:T(2,128)} %param.7) | copy-start | bytes 100
  148.1 49.9 %all-to-all-start = ((bf16[32,2,23328]{2,1,0:T(2,128)(2,1)}), bf16[32,2,23328]{2,1,0:T(2,128)(2,1)S(1)}, u32[]{:S(2)}, u32[]{:S(2)}) async-start(bf16[32,2,23328]{2,1,0:T(2,128)(2,1)} %reshape.70), calls=%async_computation | async-start | bytes 5996544 | tf_op jit(solution)/shard_map/all_to_all | solution.py:41
  333.1 16.1 %all-to-all-start.1 = ((bf16[2,32,2916]{2,0,1:T(2,128)(2,1)}), bf16[2,32,2916]{2,0,1:T(2,128)(2,1)S(1)}, u32[]{:S(2)}, u32[]{:S(2)}) async-start(bf16[2,32,2916]{2,0,1:T(2,128)(2,1)} %copy.28), calls=%async_computation.1 | async-start | bytes 753664 | tf_op jit(solution)/shard_map/all_to_all | solution.py:50
  339.1 238.8 %all-reduce.3.cloned.1.call-start = ((), (), s32[]{:S(2)}) async-start(), calls=%async_computation.2 | async-start | bytes 33030144
  350.1 5.3 copy-start
Sparse Core Ops, SparseCore 0:
  363.9 213.9 all-reduce.2
where the time goes:
time: 598 us; the launch traced here: 586 us
  local copies, waits for them, and re-layouts  284 us (47%)
  waiting for transfers between devices  258 us (43%)
  starting transfers between devices  15.7 us (3%)
  between operations  14.2 us (2%)
  matrix products  14.1 us (2%)
    unnamed x2, waiting for transfers between devices  212 us
    unnamed x11, local copies, waits for them, and re-layouts  186 us
    all_to_all x1, local copies, waits for them, and re-layouts, per_device(): lax.all_to_all(flattened, 'tm', split_axis=2, concat_axis=1, tiled=True)  92.6 us
    all_to_all x1, waiting for transfers between devices, per_device(): lax.all_to_all(flattened, 'tm', split_axis=2, concat_axis=1, tiled=True)  39.3 us
  transfers between devices with their start and end apart: 3, of which 3 were waited for; matrix products, arithmetic and copies ran while one was open for 1% of the time, Pallas kernels for 0%

commit v1 on v0

v1 whole, which is shorter than its diff:
```python
import jax
import jax.numpy as jnp
from jax import lax
from jax.experimental import pallas as pl
from jax.experimental.pallas import tpu as pltpu
from jax.sharding import PartitionSpec as P

BLOCK = 64
POOL = 8
DECAY = 16.0
F32, BF16 = jnp.float32, jnp.bfloat16
MESH = pl.DeviceIdType.MESH

D, H, TOKS = 1152, 3584, 81
ROWS = 2 * TOKS
PADDED = 176
XL = 512
YL = D - XL
CHUNK = H // 4
HALF = 512
STEP = CHUNK - HALF
SUB = 24
DY = (2, 1, 3, 0)
J2, J1, J3, J0 = 0, 1, 2, 3
C0 = 0.7978845608028654
C1 = 0.044715


def add16(a, b):
    return (a.astype(F32) + b.astype(F32)).astype(BF16)


def kernel(
    feat, wgt, cot, shots, band,
    out_proj, out_grad,
    fv, wv, cn, cv, pa, pre, kron, part, sel, pb, pt, gr,
    xa, xfu, xfd, xnu, xnd, yfu, yfd, ynu, ynd, sb, yx,
    g,
    a_fu, a_fd, a_nu, a_nd, a_1, a_gu, a_gd, a_mu, a_md, a_2, a_r,
    b_fu, b_fd, b_nu, b_nd, b_1, b_gu, b_gd, b_mu, b_md, b_2, b_r,
    c_fu, c_fd, c_nu, c_nd, c_1, c_gu, c_gd, c_mu, c_md, c_2, c_r,
    fin, fs, fr,
    local_sem, send_sem, recv_sem,
):
    dp, tm = lax.axis_index("dp"), lax.axis_index("tm")
    x_hi, core = lax.div(dp, 2), lax.rem(dp, 2)
    z, y, lo = lax.div(tm, 8), lax.rem(lax.div(tm, 2), 4), lax.rem(tm, 2)
    x = x_hi * 2 + lo

    def dev(xx=x, yy=y, zz=z, cc=core):
        return (lax.div(xx, 2) * 2 + cc, zz * 8 + yy * 2 + lax.rem(xx, 2))

    def ring(value, step):
        return lax.rem(value + step, 4)

    mate = x_hi * 2 + 1 - lo
    x_of = [ring(x, d) for d in range(4)]
    y_of = [ring(y, d) for d in range(4)]
    z_of = [ring(z, d) for d in range(4)]
    hi_of = [lax.div(v, 2) for v in x_of]
    off_of = [pl.multiple_of(lax.rem(v, 2) * STEP, 128) for v in x_of]
    cut = [pl.ds(o, HALF) for o in off_of]

    count = [0, 0]
    sends = []

    def settle():
        for copy in sends:
            copy.wait_send()
        sends.clear()

    def local(src, dst):
        i = count[0]
        count[0] += 1
        copy = pltpu.make_async_copy(src, dst, local_sem.at[i])
        copy.start()
        return copy

    def send(src, dst, to):
        i = count[1]
        count[1] += 1
        copy = pltpu.make_async_remote_copy(
            src_ref=src, dst_ref=dst, send_sem=send_sem.at[i], recv_sem=recv_sem.at[i],
            device_id=to, device_id_type=MESH,
        )
        copy.start()
        sends.append(copy)
        return copy

    la, lb = pl.ds(0, XL), pl.ds(XL, YL)
    feat_a = local(feat.at[:, :, la], fv.at[:, :, la])
    feat_b = local(feat.at[:, :, lb], fv.at[:, :, lb])

    barrier = pltpu.get_barrier_semaphore()
    group = [(lx, dy) for dy in range(4) for lx in (0, 1) if (lx, dy) != (0, 0)]
    friends = [dev(xx=mate if lx else x, yy=y_of[dy]) for lx, dy in group]
    far_x = [ring(x, 2), ring(mate, 2)]
    friends += [dev(xx=v) for v in far_x]
    friends += [dev(zz=z_of[d]) for d in (1, 2, 3)]
    friends += [dev(cc=1 - core)]
    for friend in friends:
        pl.semaphore_signal(barrier, inc=1, device_id=friend, device_id_type=MESH)

    def iota(shape, axis):
        return lax.broadcasted_iota(jnp.int32, shape, axis)

    frame, other = iota((BLOCK, 128), 0), iota((BLOCK, 128), 1)
    distance = jnp.abs(frame - other)
    decay = jnp.exp(-distance.astype(F32) / DECAY)
    ids = shots[...].astype(F32)
    ids = jnp.where(z < 2, ids[:, 0:128], ids[:, 128:256])
    ids = jnp.where(lax.rem(z, 2) == 0, ids, pltpu.roll(ids, 64, 1))
    target_of = iota((256, 128), 0)
    rel = lax.div(target_of, 32)
    target_of = lax.rem(y + lax.div(rel, 2), 4) * 2 + jnp.where(lax.rem(rel, 2) == 0, lo, 1 - lo)
    own_frame = jnp.where(iota((128, 256), 0) == (y * 2 + lo) * POOL + lax.rem(iota((128, 256), 1), 8), 1.0, 0.0)
    own_frame = own_frame.astype(BF16)
    out_row, in_row = iota((256, 256), 0), iota((256, 256), 1)
    same_token = lax.div(lax.rem(out_row, 32), 2) == lax.div(lax.rem(in_row, 128), 8)
    spread = jnp.zeros((256, 256), F32)
    for v in range(2):
        along = jnp.broadcast_to(ids[v : v + 1], (BLOCK, 128))
        down_ids = jnp.sum(jnp.where(frame == other, along, 0.0), axis=1, keepdims=True)
        allowed = (along == down_ids) & (distance <= band[v, z]) & (other < BLOCK)
        raw = jnp.where(allowed, decay, 0.0)
        mix = (raw / jnp.sum(raw, axis=1, keepdims=True)).astype(BF16).astype(F32)
        combined = (mix.reshape(8, POOL, 128).sum(axis=1) * 0.125).astype(BF16).astype(F32)
        rows = jnp.zeros((256, 128), F32)
        for p in range(8):
            rows = jnp.where(target_of == p, combined[p : p + 1], rows)
        full = jnp.dot(rows.astype(BF16), own_frame, preferred_element_type=F32)
        mine_too = same_token & (lax.rem(out_row, 2) == v) & (lax.div(in_row, 128) == v)
        spread = jnp.where(mine_too, full, spread)
    kron[...] = spread.astype(BF16)

    def partial_sums(lanes):
        for c in range(6):
            if c < 5:
                blocks = [fv[v, 128 * c : 128 * c + 128, lanes] for v in range(2)]
            else:
                empty = jnp.zeros((120, lanes.stop - lanes.start), BF16)
                blocks = [b for v in range(2) for b in (fv[v, 640:648, lanes], empty)]
            got = jnp.dot(kron[...], jnp.concatenate(blocks, axis=0), preferred_element_type=F32)
            size = 32 if c < 5 else 2
            for r in range(8):
                part[r // 2, r % 2, 32 * c : 32 * c + size, lanes] = got[32 * r : 32 * r + size].astype(BF16)

    l1, l2 = pl.ds(0, XL // 2), pl.ds(XL // 2, XL // 2)
    up, down, side, twin = dev(yy=y_of[1]), dev(yy=y_of[3]), dev(xx=mate), dev(cc=1 - core)

    feat_a.wait()
    partial_sums(slice(0, XL))
    pl.semaphore_wait(barrier, len(friends))
    x_first = {dy: send(part.at[dy, 1, :, la], xa.at[dy], side) for dy in (2, 1, 3, 0)}
    feat_b.wait()
    partial_sums(slice(XL, D))
    far_up = send(part.at[2, 0, :, lb], yfu, up)
    far_down = send(part.at[2, 1, :, lb], yfd, down)
    near_up = {1: send(part.at[1, 1, :, lb], ynu.at[1], up)}
    near_down = {0: send(part.at[3, 0, :, lb], ynd.at[0], down)}

    columns = [pl.ds(pl.multiple_of(y_of[d] * CHUNK, 128), CHUNK) for d in DY]
    cot_in = [local(cot.at[:, :, columns[j]], cn.at[j]) for j in range(4)]
    wgt_in = [local(wgt.at[:, columns[j]], wv.at[j]) for j in range(4)]

    row, col = iota((576, D), 0), iota((576, D), 1)
    wanted = row + core * 288 + jnp.where(row >= 288, 288, 0)
    sel[...] = jnp.where(col == wanted, 1.0, 0.0).astype(BF16)

    def take(dy):
        x_first[dy].wait_recv()
        xa[dy] = add16(xa[dy], part[dy, 0, :, 0:XL])

    take(2)
    far_up2 = send(xa.at[2, :, l1], xfu, up)
    far_up.wait_recv()
    yfu[...] = add16(yfu[...], part[1, 0, :, XL:D])
    near_up[0] = send(yfu, ynu.at[0], up)
    far_down.wait_recv()
    yfd[...] = add16(yfd[...], part[3, 1, :, XL:D])
    near_down[1] = send(yfd, ynd.at[1], down)
    far_down2 = send(xa.at[2, :, l2], xfd, down)
    take(1)
    near_up2 = [send(xa.at[1, :, l2], xnu.at[:, l2], up)]
    take(3)
    near_down2 = [send(xa.at[3, :, l1], xnd.at[:, l1], down)]

    for j in range(4):
        cot_in[j].wait()

        @pl.loop(0, 10)
        def _(i):
            cv[j, pl.ds(pl.multiple_of(i * 16, 16), 16), :] = cn[j, pl.ds(i * 8, 8)].reshape(16, CHUNK)

        tail = jnp.concatenate([cn[j, 80].astype(F32), jnp.zeros((14, CHUNK), F32)], axis=0)
        cv[j, 160:176, :] = tail.astype(BF16)

    far_up2.wait_recv()
    xfu[...] = add16(xfu[...], xa[1, :, 0 : XL // 2])
    near_up2.append(send(xfu, xnu.at[:, l1], up))
    near_up[1].wait_recv()
    near_down[1].wait_recv()
    sb[...] = (
        part[0, 1, :, XL:D].astype(F32) + ynu[1].astype(F32) + ynd[1].astype(F32)
    ).astype(BF16)
    last_x = send(sb, yx, side)
    far_down2.wait_recv()
    xfd[...] = add16(xfd[...], xa[3, :, XL // 2 : XL])
    near_down2.append(send(xfd, xnd.at[:, l2], down))

    def keep(value, lanes):
        value = value.astype(BF16)
        pb[0:160, lanes] = value[0:160]
        tail = jnp.concatenate(
            [value[160:162].astype(F32), jnp.zeros((14, value.shape[1]), F32)], axis=0
        )
        pb[160:176, lanes] = tail.astype(BF16)

    take(0)
    for copy in near_up2 + near_down2:
        copy.wait_recv()
    keep(xa[0].astype(F32) + xnu[...].astype(F32) + xnd[...].astype(F32), slice(0, XL))
    near_up[0].wait_recv()
    near_down[0].wait_recv()
    last_x.wait_recv()
    keep(
        part[0, 0, :, XL:D].astype(F32) + ynu[0].astype(F32) + ynd[0].astype(F32) + yx[...].astype(F32),
        slice(XL, D),
    )
    pooled_twin = send(pb.at[pl.ds(0, PADDED)], pb.at[pl.ds(PADDED, PADDED)], twin)

    grad_twin = []

    def gelu_rows(values, cotangent):
        square = values * values
        t = jnp.tanh(values * (C0 + (C0 * C1) * square))
        plus = 0.5 * (1.0 + t)
        slope = plus + (0.5 * values) * (1.0 - t * t) * (C0 + (3.0 * C0 * C1) * square)
        return (values * plus).astype(BF16), (cotangent * slope).astype(BF16)

    def forward(j):
        wgt_in[j].wait()
        pre[...] = jnp.dot(pb[0:PADDED, :], wv[j], preferred_element_type=F32)

        @pl.loop(0, 11)
        def _(i):
            rows = pl.ds(pl.multiple_of(i * 16, 16), 16)
            act, grad = gelu_rows(pre[rows, :], cv[j, rows, :].astype(F32))
            pa[j, rows, :] = act
            gr[j, rows, :] = grad

        grad_twin.append(send(gr.at[j, pl.ds(0, PADDED)], gr.at[j, pl.ds(PADDED, PADDED)], twin))

    def give(j):
        @pl.loop(0, 10)
        def _(i):
            rows = pl.ds(pl.multiple_of(i * 16, 16), 16)
            out_proj[pl.ds(i * 8, 8), :, columns[j]] = pa[j, rows, :].reshape(8, 2, CHUNK)

        out_proj[80, :, columns[j]] = pa[j, 160:162, :]

    z_up, z_down = dev(zz=z_of[1]), dev(zz=z_of[3])
    x_up, x_down = dev(xx=x_of[1]), dev(xx=x_of[3])
    zlo, zhi = pl.ds(0, 2), pl.ds(2, 2)
    msg = {}

    def backward(j):
        grad_twin[j].wait_recv()
        for h in range(2):
            got = jnp.dot(pt[288 * h : 288 * h + 288, :], gr[j], preferred_element_type=F32)
            for zz in range(4):
                for s in range(3):
                    at = zz * 72 + s * SUB
                    g[s, h, zz, j] = got[at : at + SUB].astype(BF16)
        msg["afu", j] = send(g.at[0, 0, z_of[2], j], a_fu.at[j], z_up)
        msg["afd", j] = send(g.at[0, 1, z_of[2], j], a_fd.at[j], z_down)
        msg["cfu", j] = send(g.at[2, hi_of[2], zlo, j, :, cut[2]], c_fu.at[j], x_up)
        msg["cfd", j] = send(g.at[2, hi_of[2], zhi, j, :, cut[2]], c_fd.at[j], x_down)
        if j == J2:
            msg["bfu"] = send(g.at[1, 0, :, j], b_fu, up)
            msg["bfd"] = send(g.at[1, 1, :, j], b_fd, down)
        if j == J1:
            msg["bnu1"] = send(g.at[1, 1, :, j], b_nu.at[1], up)
        if j == J3:
            msg["bnd0"] = send(g.at[1, 0, :, j], b_nd.at[0], down)
        msg["anu1", j] = send(g.at[0, 1, z_of[1], j], a_nu.at[j, 1], z_up)
        msg["and0", j] = send(g.at[0, 0, z_of[3], j], a_nd.at[j, 0], z_down)
        msg["cnu1", j] = send(g.at[2, hi_of[1], zhi, j, :, cut[1]], c_nu.at[j, zhi], x_up)
        msg["cnd0", j] = send(g.at[2, hi_of[3], zlo, j, :, cut[3]], c_nd.at[j, zlo], x_down)

    def relay(j):
        msg["afu", j].wait_recv()
        a_fu[j] = add16(a_fu[j], g[0, 0, z_of[1], j])
        msg["anu0", j] = send(a_fu.at[j], a_nu.at[j, 0], z_up)
        msg["afd", j].wait_recv()
        a_fd[j] = add16(a_fd[j], g[0, 1, z_of[3], j])
        msg["and1", j] = send(a_fd.at[j], a_nd.at[j, 1], z_down)
        msg["cfu", j].wait_recv()
        c_fu[j] = add16(c_fu[j], g[2, hi_of[1], 0:2, j, :, cut[1]])
        msg["cnu0", j] = send(c_fu.at[j], c_nu.at[j, zlo], x_up)
        msg["cfd", j].wait_recv()
        c_fd[j] = add16(c_fd[j], g[2, hi_of[3], 2:4, j, :, cut[3]])
        msg["cnd1", j] = send(c_fd.at[j], c_nd.at[j, zhi], x_down)
        if j == J1:
            msg["bfu"].wait_recv()
            b_fu[...] = add16(b_fu[...], g[1, 0, :, J1])
            msg["bnu0"] = send(b_fu, b_nu.at[0], up)
        if j == J3:
            msg["bfd"].wait_recv()
            b_fd[...] = add16(b_fd[...], g[1, 1, :, J3])
            msg["bnd1"] = send(b_fd, b_nd.at[1], down)

    forward(0)
    pooled_twin.wait_recv()
    pt[...] = lax.dot_general(
        sel[...], pb[...], (((1,), (1,)), ((), ())), preferred_element_type=F32
    ).astype(BF16)
    backward(0)
    forward(1)
    forward(2)
    backward(1)
    relay(0)
    forward(3)
    backward(2)
    relay(1)
    backward(3)
    relay(2)
    relay(3)

    def three(a, b, c):
        return (a.astype(F32) + b.astype(F32) + c.astype(F32)).astype(BF16)

    def wait(*names):
        for name in names:
            msg[name].wait_recv()

    for j in range(4):
        wait(("anu0", j), ("anu1", j), ("and0", j), ("and1", j))
        a_1[:, j] = three(g[0, :, z, j], a_nu[j], a_nd[j])
        if j == J2:
            msg["agu"] = send(a_1.at[0, j], a_gu, up)
            msg["agd"] = send(a_1.at[1, j], a_gd, down)
        if j == J1:
            msg["amu1"] = send(a_1.at[1, j], a_mu.at[1], up)
        if j == J3:
            msg["amd0"] = send(a_1.at[0, j], a_md.at[0], down)
        wait(("cnu0", j), ("cnu1", j), ("cnd0", j), ("cnd1", j))
        c_1[:, j] = three(g[2, x_hi, :, j, :, cut[0]], c_nu[j], c_nd[j])
        if j == 1:
            msg["cgu"] = send(c_1.at[z_of[2], pl.ds(0, 2)], c_gu, z_up)
            msg["cmd0"] = send(c_1.at[z_of[3], pl.ds(0, 2)], c_md.at[pl.ds(0, 2)], z_down)
        if j == 3:
            msg["cgd"] = send(c_1.at[z_of[2], pl.ds(2, 2)], c_gd, z_down)
            msg["cmu1"] = send(c_1.at[z_of[1], pl.ds(2, 2)], c_mu.at[pl.ds(2, 2)], z_up)
        if j == 2:
            give(0)
            give(1)
    wait("bnu0", "bnu1", "bnd0", "bnd1")
    b_1[...] = three(g[1, :, :, J0], b_nu[...], b_nd[...])
    msg["bgu"] = send(b_1.at[hi_of[2], zlo, :, cut[2]], b_gu, x_up)
    msg["bgd"] = send(b_1.at[hi_of[2], zhi, :, cut[2]], b_gd, x_down)
    msg["bmu1"] = send(b_1.at[hi_of[1], zhi, :, cut[1]], b_mu.at[zhi], x_up)
    msg["bmd0"] = send(b_1.at[hi_of[3], zlo, :, cut[3]], b_md.at[zlo], x_down)

    wait("agu")
    a_gu[...] = add16(a_gu[...], a_1[0, J1])
    msg["amu0"] = send(a_gu, a_mu.at[0], up)
    wait("agd")
    a_gd[...] = add16(a_gd[...], a_1[1, J3])
    msg["amd1"] = send(a_gd, a_md.at[1], down)
    wait("cgu")
    c_gu[...] = add16(c_gu[...], c_1[z_of[1], 0:2])
    msg["cmu0"] = send(c_gu, c_mu.at[pl.ds(0, 2)], z_up)
    wait("cgd")
    c_gd[...] = add16(c_gd[...], c_1[z_of[3], 2:4])
    msg["cmd1"] = send(c_gd, c_md.at[pl.ds(2, 2)], z_down)
    give(2)
    wait("bgu")
    b_gu[...] = add16(b_gu[...], b_1[hi_of[1], 0:2, :, cut[1]])
    msg["bmu0"] = send(b_gu, b_mu.at[zlo], x_up)
    wait("bgd")
    b_gd[...] = add16(b_gd[...], b_1[hi_of[3], 2:4, :, cut[3]])
    msg["bmd1"] = send(b_gd, b_md.at[zhi], x_down)

    give(3)

    wait("amu0", "amu1", "amd0", "amd1")
    a_2[...] = three(a_1[:, J0], a_mu[...], a_md[...])
    for d in (2, 1, 3):
        msg["ar", d] = send(a_2.at[hi_of[d], :, cut[d]], a_r.at[d], dev(xx=x_of[d]))
    wait("cmu0", "cmu1", "cmd0", "cmd1")
    c_2[...] = three(c_1[z], c_mu[...], c_md[...])
    for j in (J2, J1, J3):
        msg["cr", j] = send(c_2.at[j], c_r.at[j], dev(yy=y_of[DY[j]]))
    wait("bmu0", "bmu1", "bmd0", "bmd1")
    b_2[...] = three(b_1[x_hi, :, :, cut[0]], b_mu[...], b_md[...])
    for d in (2, 1, 3):
        msg["br", d] = send(b_2.at[z_of[d]], b_r.at[d], dev(zz=z_of[d]))

    def total(own, parts):
        value = own.astype(F32)
        for p in parts:
            value = value + p.astype(F32)
        return value

    settle()
    wait(("ar", 1), ("ar", 2), ("ar", 3))
    fin[0:SUB] = total(a_2[x_hi, :, cut[0]], [a_r[d] for d in (1, 2, 3)])
    wait(("cr", J1), ("cr", J2), ("cr", J3))
    fin[2 * SUB : 3 * SUB] = total(c_2[J0], [c_r[j] for j in (J1, J2, J3)])
    wait(("br", 1), ("br", 2), ("br", 3))
    fin[SUB : 2 * SUB] = total(b_2[z], [b_r[d] for d in (1, 2, 3)])

    for e in range(8):
        fs[e] = fin[9 * e : 9 * e + 9].astype(BF16)
    mine = y * 2 + lo
    for lx, dy in group:
        to_lo = 1 - lo if lx else lo
        owner = y_of[dy] * 2 + to_lo
        msg["out", lx, dy] = send(
            fs.at[owner], fr.at[lx, dy], dev(xx=mate if lx else x, yy=y_of[dy])
        )
    fr[0, 0] = fs[mine]
    for lx, dy in group:
        wait(("out", lx, dy))
    for first in (0, 1):
        for dy in range(4):
            base = y_of[(4 - dy) % 4] * CHUNK + first * STEP
            value = jnp.where(lo == first, fr[0, dy].astype(F32), fr[1, dy].astype(F32))
            out_grad[:, pl.ds(pl.multiple_of(base, 128), HALF)] = value

    settle()


def hand_over(projected, weight_grad, out_projected, out_grad, sem):
    copies = [pltpu.make_async_copy(weight_grad, out_grad, sem.at[9])]
    for i in range(9):
        rows = pl.ds(9 * i, 9)
        copies.append(pltpu.make_async_copy(projected.at[rows], out_projected.at[rows], sem.at[i]))
    for copy in copies:
        copy.start()
    for copy in copies:
        copy.wait()


N_LOCAL = 2 + 4 + 4
N_SEND = 160


def per_device(features, shot_ids, band_width, proj_weight, cotangent):
    frames = jnp.swapaxes(features, 1, 2).reshape(2, TOKS * POOL, D)
    cot = cotangent.transpose(1, 2, 0, 3).reshape(TOKS, 2, H)
    vm = lambda *shape: pltpu.VMEM(shape, BF16)
    scratch = [
        vm(2, TOKS * POOL, D), vm(4, D, CHUNK), vm(4, TOKS, 2, CHUNK), vm(4, PADDED, CHUNK),
        vm(4, PADDED, CHUNK),
        pltpu.VMEM((PADDED, CHUNK), F32), vm(256, 256), vm(4, 2, ROWS, D), vm(576, D),
        vm(2 * PADDED, D), vm(576, 2 * PADDED), vm(4, 2 * PADDED, CHUNK),
        vm(4, ROWS, XL), vm(ROWS, XL // 2), vm(ROWS, XL // 2), vm(ROWS, XL), vm(ROWS, XL),
        vm(ROWS, YL), vm(ROWS, YL), vm(2, ROWS, YL), vm(2, ROWS, YL), vm(ROWS, YL), vm(ROWS, YL),
        vm(3, 2, 4, 4, SUB, CHUNK),
        vm(4, SUB, CHUNK), vm(4, SUB, CHUNK), vm(4, 2, SUB, CHUNK), vm(4, 2, SUB, CHUNK),
        vm(2, 4, SUB, CHUNK), vm(SUB, CHUNK), vm(SUB, CHUNK), vm(2, SUB, CHUNK), vm(2, SUB, CHUNK),
        vm(2, SUB, CHUNK), vm(4, SUB, HALF),
        vm(4, SUB, CHUNK), vm(4, SUB, CHUNK), vm(2, 4, SUB, CHUNK), vm(2, 4, SUB, CHUNK),
        vm(2, 4, SUB, CHUNK), vm(2, SUB, HALF), vm(2, SUB, HALF), vm(4, SUB, HALF), vm(4, SUB, HALF),
        vm(4, SUB, HALF), vm(4, SUB, HALF),
        vm(4, 2, SUB, HALF), vm(4, 2, SUB, HALF), vm(4, 4, SUB, HALF), vm(4, 4, SUB, HALF),
        vm(4, 4, SUB, HALF), vm(2, SUB, HALF), vm(2, SUB, HALF), vm(4, SUB, HALF), vm(4, SUB, HALF),
        vm(4, SUB, HALF), vm(4, SUB, HALF),
        pltpu.VMEM((72, HALF), F32), vm(8, 9, HALF), vm(2, 4, 9, HALF),
        pltpu.SemaphoreType.DMA((N_LOCAL,)),
        pltpu.SemaphoreType.DMA((N_SEND,)),
        pltpu.SemaphoreType.DMA((N_SEND,)),
    ]
    any_spec = pl.BlockSpec(memory_space=pl.ANY)
    vmem_spec = pl.BlockSpec(memory_space=pltpu.VMEM)
    smem_spec = pl.BlockSpec(memory_space=pltpu.SMEM)
    projected, weight_grad = pl.pallas_call(
        kernel,
        out_shape=(
            pltpu.VMEM(cot.shape, BF16),
            pltpu.VMEM((9, H), F32),
        ),
        in_specs=[any_spec, any_spec, any_spec, vmem_spec, smem_spec],
        out_specs=(vmem_spec, vmem_spec),
        scratch_shapes=scratch,
        compiler_params=pltpu.CompilerParams(
            collective_id=0, has_side_effects=True, vmem_limit_bytes=50 * 1024 * 1024
        ),
        cost_estimate=pl.CostEstimate(flops=4 * 10**9, bytes_accessed=14 * 10**6, transcendentals=600000),
    )(frames, proj_weight, cot, shot_ids, band_width)
    projected, weight_grad = pl.pallas_call(
        hand_over,
        out_shape=(
            jax.ShapeDtypeStruct(projected.shape, BF16),
            jax.ShapeDtypeStruct(weight_grad.shape, F32),
        ),
        in_specs=[vmem_spec, vmem_spec],
        out_specs=(any_spec, any_spec),
        scratch_shapes=[pltpu.SemaphoreType.DMA((10,))],
    )(projected, weight_grad)
    return projected.reshape(1, TOKS, 2, H).transpose(2, 0, 1, 3), weight_grad


def solution(mesh):
    return jax.shard_map(
        per_device,
        mesh=mesh,
        in_specs=(
            P("dp", "tm", None, None),
            P("dp", None),
            P("dp", None),
            P(),
            P("dp", "tm", None, None),
        ),
        out_specs=(P("dp", "tm", None, None), P(("dp", "tm"), None)),
        check_vma=False,
    )
```

time: 598 us -> 78.1 us (0.13); the launches traced: 586 us -> 77.8 us
  local copies, waits for them, and re-layouts: 284 us -> 4.32 us
  waiting for transfers between devices: 258 us -> 0 us
  Pallas kernels: 0 us -> 72.9 us
  starting transfers between devices: 15.7 us -> 0 us
  matrix products: 14.1 us -> 0 us
  between operations: 14.2 us -> 0.66 us
    unnamed x2 -> x0, waiting for transfers between devices: 212 us -> none
    unnamed x11 -> x10, local copies, waits for them, and re-layouts: 186 us -> 4.32 us
    all_to_all x2 -> x0, local copies, waits for them, and re-layouts: 92.6 us -> none  [the longest x1 92.6 us: per_device(): lax.all_to_all(flattened, 'tm', split_axis=2, concat_axis=1, tiled=True)]
    pallas_call x0 -> x2, Pallas kernels: none -> 72.9 us  [the longest x1 70.4 us: per_device(): pl.pallas_call(kernel, out_shape=(pltpu.VMEM(cot.shape, BF16), pltpu.VMEM...]
    all_to_all x2 -> x0, waiting for transfers between devices: 45.9 us -> none  [the longest x1 39.3 us: per_device(): lax.all_to_all(flattened, 'tm', split_axis=2, concat_axis=1, tiled=True)]
    all_to_all x2 -> x0, starting transfers between devices: 15.5 us -> none  [the longest x1 9.48 us: per_device(): lax.all_to_all(flattened, 'tm', split_axis=2, concat_axis=1, tiled=True)]
    dot_general x3 -> x0, matrix products: 14.1 us -> none  [the longest x1 8.26 us: per_device(): jnp.einsum('rd,rh->dh', pooled_rows, grad_preact, preferred_element_type=...]
  transfers between devices with their start and end apart: 3 -> 0, of which waited for: 3 -> 0; matrix products, arithmetic and copies ran while one was open for 1% -> 0% of each run, Pallas kernels for 0% -> 0%
where the time goes in v1:
time: 78.1 us; the launch traced here: 77.8 us
  Pallas kernels  72.9 us (93%)
  local copies, waits for them, and re-layouts  4.32 us (6%)
    pallas_call x1, Pallas kernels, per_device(): pl.pallas_call(kernel, out_shape=(pltpu.VMEM(cot.shape, BF16), pltpu.VMEM...  70.4 us
    unnamed x10, local copies, waits for them, and re-layouts  4.32 us
    pallas_call x1, Pallas kernels, per_device(): pl.pallas_call(hand_over, out_shape=(jax.ShapeDtypeStruct(projected.shape...  2.44 us

profile of v1, /device:TPU:0, one launch (start us, length us, event | category | flops | bytes accessed | tf_op | source)
XLA Modules:
  0.0 77.8 jit_solution(4692882045677705901)
XLA Ops:
  0.6 0.0 copy-start.2
  0.6 1.3 %copy-done.2 = bf16[2,1,81,3584]{3,0,2,1:T(2,128)(2,1)S(1)} copy-done((bf16[2,1,81,3584]{3,0,2,1:T(2,128)(2,1)S(1)}, bf16[2,1,81,3584]{3,0,2,1:T(2,128)(2,1)}, u32[]{:S(2)}) %copy-start.2) | copy-done | bytes 1161240
  1.9 0.0 copy-start.3
  1.9 0.7 copy-done.3
  2.6 0.0 copy-start.4
  2.6 0.7 copy-done.4
  3.3 70.4 %shard_map.68 = (bf16[81,2,3584]{2,1,0:T(2,128)(2,1)S(1)}, f32[9,3584]{1,0:T(8,128)S(1)}) custom-call(bf16[2,648,1152]{2,1,0:T(8,128)(2,1)} %bitcast.10, bf16[1152,3584]{1,0:T(8,128)(2,1)} %wgt.1, bf16[81,2,3584]{2,1,0:T(2,128)(2,1)S(1)} %bitcast.9, s32[2,256]{1,0:T(2,128)S(1)} %copy-done.3, s32[2,4]{1,0:T(2,128)S(1)} %copy-done.4), custom_call_target="tpu_custom_call" | custom-call | flops 4000000000 | bytes 14000000 | tf_op jit(solution)/shard_map/pallas_call | solution.py:479
  73.7 0.0 copy-start
  73.7 1.0 %copy-done = bf16[81,2,3584]{2,1,0:T(2,128)(2,1)} copy-done((bf16[81,2,3584]{2,1,0:T(2,128)(2,1)}, bf16[81,2,3584]{2,1,0:T(2,128)(2,1)S(1)}, u32[]{:S(2)}) %copy-start) | copy-done | bytes 1161240
  74.7 0.0 copy-start.1
  74.7 0.7 copy-done.1
  75.4 2.4 %shard_map.69 = (bf16[81,2,3584]{2,1,0:T(2,128)(2,1)}, f32[9,3584]{1,0:T(8,128)}) custom-call(bf16[81,2,3584]{2,1,0:T(2,128)(2,1)} %copy-done, f32[9,3584]{1,0:T(8,128)} %copy-done.1), custom_call_target="tpu_custom_call" | custom-call | tf_op jit(solution)/shard_map/pallas_call | solution.py:493
Async XLA Ops:
  0.6 1.3 %copy-start.2 = (bf16[2,1,81,3584]{3,0,2,1:T(2,128)(2,1)S(1)}, bf16[2,1,81,3584]{3,0,2,1:T(2,128)(2,1)}, u32[]{:S(2)}) copy-start(bf16[2,1,81,3584]{3,0,2,1:T(2,128)(2,1)} %param.9) | copy-start | bytes 3483652
  1.9 0.7 copy-start.3
  2.6 0.7 copy-start.4
  73.7 1.0 %copy-start = (bf16[81,2,3584]{2,1,0:T(2,128)(2,1)}, bf16[81,2,3584]{2,1,0:T(2,128)(2,1)S(1)}, u32[]{:S(2)}) copy-start(bf16[81,2,3584]{2,1,0:T(2,128)(2,1)S(1)} %get-tuple-element.6.projected) | copy-start | bytes 3483652
  74.7 0.7 copy-start.1

commit v2 on v1

v2 whole, which is shorter than its diff:
```python
import jax
import jax.numpy as jnp
from jax import lax
from jax.experimental import pallas as pl
from jax.experimental.pallas import tpu as pltpu
from jax.sharding import PartitionSpec as P

BLOCK = 64
POOL = 8
DECAY = 16.0
F32, BF16 = jnp.float32, jnp.bfloat16
MESH = pl.DeviceIdType.MESH

D, H, TOKS = 1152, 3584, 81
ROWS = 2 * TOKS
PADDED = 176
XL = 512
YL = D - XL
CHUNK = H // 4
ORDER = (("z", "y", "x"), ("y", "x", "z"), ("x", "z", "y"))
S1, S2, S3 = 24, 12, 3
C0 = 0.7978845608028654
C1 = 0.044715


def add16(a, b):
    return (a.astype(F32) + b.astype(F32)).astype(BF16)


def kernel(
    feat, wgt, cot, shots_in, band_in,
    out_proj, out_grad,
    fv, wv, cn, cv, pa, pre, kron, part, sel, pb, pt, gr,
    xa, xfu, xfd, xnu, xnd, yfu, yfd, ynu, ynd, sb, yx,
    g,
    fu, fd, nu, nd, r1, fu2, fd2, nu2, nd2, r2, r3,
    ids_v, band_s,
    local_sem, send_sem, recv_sem,
):
    dp, tm = lax.axis_index("dp"), lax.axis_index("tm")
    x_hi, core = lax.div(dp, 2), lax.rem(dp, 2)
    z, y, lo = lax.div(tm, 8), lax.rem(lax.div(tm, 2), 4), lax.rem(tm, 2)
    x = x_hi * 2 + lo

    def dev(xx=x, yy=y, zz=z, cc=core):
        return (lax.div(xx, 2) * 2 + cc, zz * 8 + yy * 2 + lax.rem(xx, 2))

    def ring(value, step):
        return lax.rem(value + step, 4)

    mate = x_hi * 2 + 1 - lo
    here = {"x": x, "y": y, "z": z}
    index = {axis: [ring(here[axis], d) for d in range(4)] for axis in "xyz"}
    hop = {axis: [dev(**{axis * 2: index[axis][d]}) for d in range(4)] for axis in "xyz"}

    count = [0, 0]
    sends = []

    def settle():
        for copy in sends:
            copy.wait_send()
        sends.clear()

    def local(src, dst):
        i = count[0]
        count[0] += 1
        copy = pltpu.make_async_copy(src, dst, local_sem.at[i])
        copy.start()
        return copy

    def send(src, dst, to):
        i = count[1]
        count[1] += 1
        copy = pltpu.make_async_remote_copy(
            src_ref=src, dst_ref=dst, send_sem=send_sem.at[i], recv_sem=recv_sem.at[i],
            device_id=to, device_id_type=MESH,
        )
        copy.start()
        sends.append(copy)
        return copy

    la, lb = pl.ds(0, XL), pl.ds(XL, YL)
    ids_in = local(shots_in, ids_v)
    width_in = local(band_in, band_s)
    feat_a = local(feat.at[:, :, la], fv.at[:, :, la])
    feat_b = local(feat.at[:, :, lb], fv.at[:, :, lb])

    barrier = pltpu.get_barrier_semaphore()
    friends = [hop[axis][d] for axis in "xyz" for d in (1, 2, 3)] + [dev(cc=1 - core)]
    for friend in friends:
        pl.semaphore_signal(barrier, inc=1, device_id=friend, device_id_type=MESH)

    def iota(shape, axis):
        return lax.broadcasted_iota(jnp.int32, shape, axis)

    frame, other = iota((BLOCK, 128), 0), iota((BLOCK, 128), 1)
    distance = jnp.abs(frame - other)
    decay = jnp.exp(-distance.astype(F32) / DECAY)
    ids_in.wait()
    width_in.wait()
    ids = ids_v[...].astype(F32)
    ids = jnp.where(z < 2, ids[:, 0:128], ids[:, 128:256])
    ids = jnp.where(lax.rem(z, 2) == 0, ids, pltpu.roll(ids, 64, 1))
    target_of = iota((256, 128), 0)
    rel = lax.div(target_of, 32)
    target_of = lax.rem(y + lax.div(rel, 2), 4) * 2 + jnp.where(lax.rem(rel, 2) == 0, lo, 1 - lo)
    own_frame = jnp.where(iota((128, 256), 0) == (y * 2 + lo) * POOL + lax.rem(iota((128, 256), 1), 8), 1.0, 0.0)
    own_frame = own_frame.astype(BF16)
    out_row, in_row = iota((256, 256), 0), iota((256, 256), 1)
    same_token = lax.div(lax.rem(out_row, 32), 2) == lax.div(lax.rem(in_row, 128), 8)
    spread = jnp.zeros((256, 256), F32)
    for v in range(2):
        along = jnp.broadcast_to(ids[v : v + 1], (BLOCK, 128))
        down_ids = jnp.sum(jnp.where(frame == other, along, 0.0), axis=1, keepdims=True)
        allowed = (along == down_ids) & (distance <= band_s[v, z]) & (other < BLOCK)
        raw = jnp.where(allowed, decay, 0.0)
        mix = (raw / jnp.sum(raw, axis=1, keepdims=True)).astype(BF16).astype(F32)
        combined = (mix.reshape(8, POOL, 128).sum(axis=1) * 0.125).astype(BF16).astype(F32)
        rows = jnp.zeros((256, 128), F32)
        for p in range(8):
            rows = jnp.where(target_of == p, combined[p : p + 1], rows)
        full = jnp.dot(rows.astype(BF16), own_frame, preferred_element_type=F32)
        mine_too = same_token & (lax.rem(out_row, 2) == v) & (lax.div(in_row, 128) == v)
        spread = jnp.where(mine_too, full, spread)
    kron[...] = spread.astype(BF16)

    def partial_sums(lanes):
        for c in range(6):
            if c < 5:
                blocks = [fv[v, 128 * c : 128 * c + 128, lanes] for v in range(2)]
            else:
                empty = jnp.zeros((120, lanes.stop - lanes.start), BF16)
                blocks = [b for v in range(2) for b in (fv[v, 640:648, lanes], empty)]
            got = jnp.dot(kron[...], jnp.concatenate(blocks, axis=0), preferred_element_type=F32)
            size = 32 if c < 5 else 2
            for r in range(8):
                part[r // 2, r % 2, 32 * c : 32 * c + size, lanes] = got[32 * r : 32 * r + size].astype(BF16)

    l1, l2 = pl.ds(0, XL // 2), pl.ds(XL // 2, XL // 2)
    up, down, side, twin = hop["y"][1], hop["y"][3], dev(xx=mate), dev(cc=1 - core)

    feat_a.wait()
    partial_sums(slice(0, XL))
    pl.semaphore_wait(barrier, len(friends))
    x_first = {dy: send(part.at[dy, 1, :, la], xa.at[dy], side) for dy in (2, 1, 3, 0)}
    feat_b.wait()
    partial_sums(slice(XL, D))
    far_up = send(part.at[2, 0, :, lb], yfu, up)
    far_down = send(part.at[2, 1, :, lb], yfd, down)
    near_up = {1: send(part.at[1, 1, :, lb], ynu.at[1], up)}
    near_down = {0: send(part.at[3, 0, :, lb], ynd.at[0], down)}

    columns = [pl.ds(j * CHUNK, CHUNK) for j in range(4)]
    cot_in = [local(cot.at[:, :, columns[j]], cn.at[j]) for j in range(4)]
    wgt_in = [local(wgt.at[:, columns[j]], wv.at[j]) for j in range(4)]

    row, lane = iota((576, 128), 0), iota((576, 128), 1)
    which = lax.div(row, 192)
    first, second, third = lax.div(lax.rem(row, 192), 48), lax.div(lax.rem(row, 48), 12), lax.div(lax.rem(row, 12), 3)
    at = {}
    for axis in "xyz":
        at[axis] = jnp.zeros((576, 128), jnp.int32)
        for s in range(3):
            place = (first, second, third)[ORDER[s].index(axis)]
            at[axis] = jnp.where(which == s, place, at[axis])
    owner = (lax.div(at["x"], 2) * 2 + core) * 32 + at["z"] * 8 + at["y"] * 2 + lax.rem(at["x"], 2)
    wanted = owner * 9 + which * S3 + lax.rem(row, S3)
    for k in range(D // 128):
        sel[:, 128 * k : 128 * k + 128] = jnp.where(wanted == lane + 128 * k, 1.0, 0.0).astype(BF16)

    def take(dy):
        x_first[dy].wait_recv()
        xa[dy] = add16(xa[dy], part[dy, 0, :, 0:XL])

    take(2)
    far_up2 = send(xa.at[2, :, l1], xfu, up)
    far_up.wait_recv()
    yfu[...] = add16(yfu[...], part[1, 0, :, XL:D])
    near_up[0] = send(yfu, ynu.at[0], up)
    far_down.wait_recv()
    yfd[...] = add16(yfd[...], part[3, 1, :, XL:D])
    near_down[1] = send(yfd, ynd.at[1], down)
    far_down2 = send(xa.at[2, :, l2], xfd, down)
    take(1)
    near_up2 = [send(xa.at[1, :, l2], xnu.at[:, l2], up)]
    take(3)
    near_down2 = [send(xa.at[3, :, l1], xnd.at[:, l1], down)]

    for j in range(4):
        cot_in[j].wait()

        @pl.loop(0, 10)
        def _(i):
            cv[j, pl.ds(pl.multiple_of(i * 16, 16), 16), :] = cn[j, pl.ds(i * 8, 8)].reshape(16, CHUNK)

        tail = jnp.concatenate([cn[j, 80].astype(F32), jnp.zeros((14, CHUNK), F32)], axis=0)
        cv[j, 160:176, :] = tail.astype(BF16)

    far_up2.wait_recv()
    xfu[...] = add16(xfu[...], xa[1, :, 0 : XL // 2])
    near_up2.append(send(xfu, xnu.at[:, l1], up))
    near_up[1].wait_recv()
    near_down[1].wait_recv()
    sb[...] = (
        part[0, 1, :, XL:D].astype(F32) + ynu[1].astype(F32) + ynd[1].astype(F32)
    ).astype(BF16)
    last_x = send(sb, yx, side)
    far_down2.wait_recv()
    xfd[...] = add16(xfd[...], xa[3, :, XL // 2 : XL])
    near_down2.append(send(xfd, xnd.at[:, l2], down))

    def keep(value, lanes):
        value = value.astype(BF16)
        pb[0:160, lanes] = value[0:160]
        tail = jnp.concatenate(
            [value[160:162].astype(F32), jnp.zeros((14, value.shape[1]), F32)], axis=0
        )
        pb[160:176, lanes] = tail.astype(BF16)

    take(0)
    for copy in near_up2 + near_down2:
        copy.wait_recv()
    keep(xa[0].astype(F32) + xnu[...].astype(F32) + xnd[...].astype(F32), slice(0, XL))
    near_up[0].wait_recv()
    near_down[0].wait_recv()
    last_x.wait_recv()
    keep(
        part[0, 0, :, XL:D].astype(F32) + ynu[0].astype(F32) + ynd[0].astype(F32) + yx[...].astype(F32),
        slice(XL, D),
    )
    pooled_twin = send(pb.at[pl.ds(0, PADDED)], pb.at[pl.ds(PADDED, PADDED)], twin)

    grad_twin = []

    def gelu_rows(values, cotangent):
        square = values * values
        t = jnp.tanh(values * (C0 + (C0 * C1) * square))
        plus = 0.5 * (1.0 + t)
        slope = plus + (0.5 * values) * (1.0 - t * t) * (C0 + (3.0 * C0 * C1) * square)
        return (values * plus).astype(BF16), (cotangent * slope).astype(BF16)

    def forward(j):
        wgt_in[j].wait()
        pre[...] = jnp.dot(pb[0:PADDED, :], wv[j], preferred_element_type=F32)

        @pl.loop(0, 11)
        def _(i):
            rows = pl.ds(pl.multiple_of(i * 16, 16), 16)
            act, grad = gelu_rows(pre[rows, :], cv[j, rows, :].astype(F32))
            pa[j, rows, :] = act
            gr[j, rows, :] = grad

        grad_twin.append(send(gr.at[j, pl.ds(0, PADDED)], gr.at[j, pl.ds(PADDED, PADDED)], twin))

    def give(j):
        @pl.loop(0, 10)
        def _(i):
            rows = pl.ds(pl.multiple_of(i * 16, 16), 16)
            out_proj[pl.ds(i * 8, 8), :, columns[j]] = pa[j, rows, :].reshape(8, 2, CHUNK)

        out_proj[80, :, columns[j]] = pa[j, 160:162, :]

    msg = {}

    def wait(*names):
        for name in names:
            msg[name].wait_recv()

    def add3(a, b, c):
        return a.astype(F32) + b.astype(F32) + c.astype(F32)

    def backward(j):
        grad_twin[j].wait_recv()
        got = jnp.dot(pt[...], gr[j], preferred_element_type=F32)
        for s in range(3):
            for a in range(4):
                for h in range(2):
                    base = s * 192 + a * 48 + h * S1
                    g[s, a, h, j] = got[base : base + S1].astype(BF16)
        for s in range(3):
            i, to = index[ORDER[s][0]], hop[ORDER[s][0]]
            msg["fu", s, j] = send(g.at[s, i[2], 0, j], fu.at[s, j], to[1])
            msg["fd", s, j] = send(g.at[s, i[2], 1, j], fd.at[s, j], to[3])
        for s in range(3):
            i, to = index[ORDER[s][0]], hop[ORDER[s][0]]
            msg["nu1", s, j] = send(g.at[s, i[1], 1, j], nu.at[s, j, 1], to[1])
            msg["nd0", s, j] = send(g.at[s, i[3], 0, j], nd.at[s, j, 0], to[3])

    def relay(j):
        for s in range(3):
            i, to = index[ORDER[s][0]], hop[ORDER[s][0]]
            wait(("fu", s, j))
            fu[s, j] = add16(fu[s, j], g[s, i[1], 0, j])
            msg["nu0", s, j] = send(fu.at[s, j], nu.at[s, j, 0], to[1])
            wait(("fd", s, j))
            fd[s, j] = add16(fd[s, j], g[s, i[3], 1, j])
            msg["nd1", s, j] = send(fd.at[s, j], nd.at[s, j, 1], to[3])

    def finish(j):
        for s in range(3):
            i = index[ORDER[s][0]]
            wait(("nu1", s, j), ("nd0", s, j), ("nu0", s, j), ("nd1", s, j))
            value = add3(g[s, i[0], :, j], nu[s, j], nd[s, j]).reshape(2 * S1, CHUNK)
            for b in range(4):
                r1[s, b, j] = value[S2 * b : S2 * b + S2].astype(BF16)

    def second_stage(q):
        for s in range(3):
            i, to = index[ORDER[s][1]], hop[ORDER[s][1]]
            msg["fu2", s, q] = send(r1.at[s, i[2], 2 * q], fu2.at[s, q], to[1])
            msg["fd2", s, q] = send(r1.at[s, i[2], 2 * q + 1], fd2.at[s, q], to[3])
        for s in range(3):
            i, to = index[ORDER[s][1]], hop[ORDER[s][1]]
            msg["mu1", s, q] = send(r1.at[s, i[1], 2 * q + 1], nu2.at[s, q, 1], to[1])
            msg["md0", s, q] = send(r1.at[s, i[3], 2 * q], nd2.at[s, q, 0], to[3])

    def second_relay(q):
        for s in range(3):
            i, to = index[ORDER[s][1]], hop[ORDER[s][1]]
            wait(("fu2", s, q))
            fu2[s, q] = add16(fu2[s, q], r1[s, i[1], 2 * q])
            msg["mu0", s, q] = send(fu2.at[s, q], nu2.at[s, q, 0], to[1])
            wait(("fd2", s, q))
            fd2[s, q] = add16(fd2[s, q], r1[s, i[3], 2 * q + 1])
            msg["md1", s, q] = send(fd2.at[s, q], nd2.at[s, q, 1], to[3])

    def third_stage(q):
        for s in range(3):
            i = index[ORDER[s][1]]
            wait(("mu1", s, q), ("md0", s, q), ("mu0", s, q), ("md1", s, q))
            for k in range(2):
                value = add3(r1[s, i[0], 2 * q + k], nu2[s, q, k], nd2[s, q, k])
                for c in range(4):
                    r2[s, c, q, k] = value[S3 * c : S3 * c + S3].astype(BF16)
            i, to = index[ORDER[s][2]], hop[ORDER[s][2]]
            for d in (2, 1, 3):
                msg["last", s, q, d] = send(r2.at[s, i[d], q], r3.at[s, d, q], to[d])

    def owned(q):
        for s in range(3):
            i = index[ORDER[s][2]]
            wait(*(("last", s, q, d) for d in (1, 2, 3)))
            for k in range(2):
                total = r2[s, i[0], q, k].astype(F32)
                for d in (1, 2, 3):
                    total = total + r3[s, d, q, k].astype(F32)
                base = (2 * q + k) * CHUNK
                out_grad[S3 * s : S3 * s + S3, base : base + CHUNK] = total

    forward(0)
    pooled_twin.wait_recv()
    pt[...] = lax.dot_general(
        sel[...], pb[...], (((1,), (1,)), ((), ())), preferred_element_type=F32
    ).astype(BF16)
    backward(0)
    forward(1)
    forward(2)
    backward(1)
    relay(0)
    forward(3)
    backward(2)
    relay(1)
    backward(3)
    relay(2)
    finish(0)
    relay(3)
    finish(1)
    second_stage(0)
    give(0)
    finish(2)
    second_relay(0)
    finish(3)
    second_stage(1)
    give(1)
    third_stage(0)
    give(2)
    second_relay(1)
    give(3)
    settle()
    third_stage(1)
    owned(0)
    owned(1)
    settle()


def hand_over(projected, weight_grad, out_projected, out_grad, sem):
    copies = [pltpu.make_async_copy(weight_grad, out_grad, sem.at[9])]
    for i in range(9):
        rows = pl.ds(9 * i, 9)
        copies.append(pltpu.make_async_copy(projected.at[rows], out_projected.at[rows], sem.at[i]))
    for copy in copies:
        copy.start()
    for copy in copies:
        copy.wait()


N_LOCAL = 4 + 4 + 4
N_SEND = 160


def per_device(features, shot_ids, band_width, proj_weight, cotangent):
    frames = jnp.swapaxes(features, 1, 2).reshape(2, TOKS * POOL, D)
    cot = cotangent.transpose(1, 2, 0, 3).reshape(TOKS, 2, H)
    vm = lambda *shape: pltpu.VMEM(shape, BF16)
    scratch = [
        vm(2, TOKS * POOL, D), vm(4, D, CHUNK), vm(4, TOKS, 2, CHUNK), vm(4, PADDED, CHUNK),
        vm(4, PADDED, CHUNK),
        pltpu.VMEM((PADDED, CHUNK), F32), vm(256, 256), vm(4, 2, ROWS, D), vm(576, D),
        vm(2 * PADDED, D), vm(576, 2 * PADDED), vm(4, 2 * PADDED, CHUNK),
        vm(4, ROWS, XL), vm(ROWS, XL // 2), vm(ROWS, XL // 2), vm(ROWS, XL), vm(ROWS, XL),
        vm(ROWS, YL), vm(ROWS, YL), vm(2, ROWS, YL), vm(2, ROWS, YL), vm(ROWS, YL), vm(ROWS, YL),
        vm(3, 4, 2, 4, S1, CHUNK),
        vm(3, 4, S1, CHUNK), vm(3, 4, S1, CHUNK), vm(3, 4, 2, S1, CHUNK), vm(3, 4, 2, S1, CHUNK),
        vm(3, 4, 4, S2, CHUNK), vm(3, 2, S2, CHUNK), vm(3, 2, S2, CHUNK),
        vm(3, 2, 2, S2, CHUNK), vm(3, 2, 2, S2, CHUNK),
        vm(3, 4, 2, 2, S3, CHUNK), vm(3, 4, 2, 2, S3, CHUNK),
        pltpu.VMEM(shot_ids.shape, jnp.int32), pltpu.SMEM(band_width.shape, jnp.int32),
        pltpu.SemaphoreType.DMA((N_LOCAL,)),
        pltpu.SemaphoreType.DMA((N_SEND,)),
        pltpu.SemaphoreType.DMA((N_SEND,)),
    ]
    any_spec = pl.BlockSpec(memory_space=pl.ANY)
    vmem_spec = pl.BlockSpec(memory_space=pltpu.VMEM)
    inputs = [
        pltpu.with_memory_space_constraint(a, pltpu.HBM)
        for a in (frames, proj_weight, cot, shot_ids, band_width)
    ]
    projected, weight_grad = pl.pallas_call(
        kernel,
        out_shape=(
            pltpu.VMEM(cot.shape, BF16),
            pltpu.VMEM((9, H), F32),
        ),
        in_specs=[any_spec] * 5,
        out_specs=(vmem_spec, vmem_spec),
        scratch_shapes=scratch,
        compiler_params=pltpu.CompilerParams(
            collective_id=0, has_side_effects=True, vmem_limit_bytes=50 * 1024 * 1024
        ),
        cost_estimate=pl.CostEstimate(flops=4 * 10**9, bytes_accessed=14 * 10**6, transcendentals=600000),
    )(*inputs)
    projected, weight_grad = pl.pallas_call(
        hand_over,
        out_shape=(
            jax.ShapeDtypeStruct(projected.shape, BF16),
            jax.ShapeDtypeStruct(weight_grad.shape, F32),
        ),
        in_specs=[vmem_spec, vmem_spec],
        out_specs=(any_spec, any_spec),
        scratch_shapes=[pltpu.SemaphoreType.DMA((10,))],
    )(*(pltpu.with_memory_space_constraint(a, pltpu.VMEM) for a in (projected, weight_grad)))
    return projected.reshape(1, TOKS, 2, H).transpose(2, 0, 1, 3), weight_grad


def solution(mesh):
    return jax.shard_map(
        per_device,
        mesh=mesh,
        in_specs=(
            P("dp", "tm", None, None),
            P("dp", None),
            P("dp", None),
            P(),
            P("dp", "tm", None, None),
        ),
        out_specs=(P("dp", "tm", None, None), P(("dp", "tm"), None)),
        check_vma=False,
    )
```

time: 78.1 us -> 66.7 us (0.85)
  Pallas kernels: 72.9 us -> 65.9 us
  local copies, waits for them, and re-layouts: 4.32 us -> 0 us
    pallas_call x1, Pallas kernels: 70.4 us -> 64.7 us  [per_device(): pl.pallas_call(kernel, out_shape=(pltpu.VMEM(cot.shape, BF16), pltpu.VMEM...]
    unnamed x10 -> x0, local copies, waits for them, and re-layouts: 4.32 us -> none
    pallas_call x1, Pallas kernels: 2.44 us -> 1.15 us  [per_device(): pl.pallas_call(hand_over, out_shape=(jax.ShapeDtypeStruct(projected.shape...]
where the time goes in v2:
time: 66.7 us; the launch traced here: 66.5 us
  Pallas kernels  65.9 us (99%)
    pallas_call x1, Pallas kernels, per_device(): pl.pallas_call(kernel, out_shape=(pltpu.VMEM(cot.shape, BF16), pltpu.VMEM...  64.7 us

profile of v2, /device:TPU:0, one launch (start us, length us, event | category | flops | bytes accessed | tf_op | source)
XLA Modules:
  0.0 66.5 jit_solution(16141263836784096666)
XLA Ops:
  0.6 64.7 %shard_map.68 = (bf16[81,2,3584]{2,1,0:T(2,128)(2,1)S(1)}, f32[9,3584]{1,0:T(8,128)S(1)}) custom-call(bf16[2,648,1152]{2,1,0:T(8,128)(2,1)} %bitcast.9, bf16[1152,3584]{1,0:T(8,128)(2,1)} %wgt.1, bf16[81,2,3584]{2,1,0:T(2,128)(2,1)} %bitcast.10, s32[2,256]{1,0:T(2,128)} %shots_in.1, s32[2,4]{1,0:T(2,128)} %band_in.1), custom_call_target="tpu_custom_call" | custom-call | flops 4000000000 | bytes 14000000 | tf_op jit(solution)/shard_map/pallas_call | solution.py:428
  65.4 1.2 %shard_map.69 = (bf16[81,2,3584]{2,1,0:T(2,128)(2,1)}, f32[9,3584]{1,0:T(8,128)}) custom-call(bf16[81,2,3584]{2,1,0:T(2,128)(2,1)S(1)} %get-tuple-element.6.projected, f32[9,3584]{1,0:T(8,128)S(1)} %get-tuple-element.7.weight_grad), custom_call_target="tpu_custom_call" | custom-call | tf_op jit(solution)/shard_map/pallas_call | solution.py:442

commit v3 on v2

--- a/solution.py
+++ b/solution.py
@@ -27,71 +27,81 @@
     return (a.astype(F32) + b.astype(F32)).astype(BF16)
 
 
-def kernel(
+class Place:
+    def __init__(self, local_sem, send_sem, recv_sem):
+        dp, tm = lax.axis_index("dp"), lax.axis_index("tm")
+        self.core = lax.rem(dp, 2)
+        self.lo = lax.rem(tm, 2)
+        self.z, self.y = lax.div(tm, 8), lax.rem(lax.div(tm, 2), 4)
+        self.x = lax.div(dp, 2) * 2 + self.lo
+        here = {"x": self.x, "y": self.y, "z": self.z}
+        self.index = {a: [lax.rem(here[a] + d, 4) for d in range(4)] for a in "xyz"}
+        self.hop = {a: [self.dev(**{a: self.index[a][d]}) for d in range(4)] for a in "xyz"}
+        self.mate = self.dev(x=self.x + 1 - 2 * self.lo)
+        self.twin = self.dev(core=1 - self.core)
+        self.sems = local_sem, send_sem, recv_sem
+        self.count = [0, 0]
+        self.sends = []
+
+    def dev(self, x=None, y=None, z=None, core=None):
+        x, y, z, core = (
+            mine if other is None else other
+            for other, mine in ((x, self.x), (y, self.y), (z, self.z), (core, self.core))
+        )
+        return (lax.div(x, 2) * 2 + core, z * 8 + y * 2 + lax.rem(x, 2))
+
+    def greet(self, friends):
+        barrier = pltpu.get_barrier_semaphore()
+        for friend in friends:
+            pl.semaphore_signal(barrier, inc=1, device_id=friend, device_id_type=MESH)
+        return lambda: pl.semaphore_wait(barrier, len(friends))
+
+    def local(self, src, dst):
+        i = self.count[0]
+        self.count[0] += 1
+        copy = pltpu.make_async_copy(src, dst, self.sems[0].at[i])
+        copy.start()
+        return copy
+
+    def send(self, src, dst, to):
+        i = self.count[1]
+        self.count[1] += 1
+        copy = pltpu.make_async_remote_copy(
+            src_ref=src, dst_ref=dst, send_sem=self.sems[1].at[i], recv_sem=self.sems[2].at[i],
+            device_id=to, device_id_type=MESH,
+        )
+        copy.start()
+        self.sends.append(copy)
+        return copy
+
+    def settle(self):
+        for copy in self.sends:
+            copy.wait_send()
+        self.sends.clear()
+
+
+def iota(shape, axis):
+    return lax.broadcasted_iota(jnp.int32, shape, axis)
+
+
+def pool_kernel(
     feat, wgt, cot, shots_in, band_in,
-    out_proj, out_grad,
-    fv, wv, cn, cv, pa, pre, kron, part, sel, pb, pt, gr,
+    pb, wv, cv, sel,
+    fv, cn, kron, part,
     xa, xfu, xfd, xnu, xnd, yfu, yfd, ynu, ynd, sb, yx,
-    g,
-    fu, fd, nu, nd, r1, fu2, fd2, nu2, nd2, r2, r3,
     ids_v, band_s,
     local_sem, send_sem, recv_sem,
 ):
-    dp, tm = lax.axis_index("dp"), lax.axis_index("tm")
-    x_hi, core = lax.div(dp, 2), lax.rem(dp, 2)
-    z, y, lo = lax.div(tm, 8), lax.rem(lax.div(tm, 2), 4), lax.rem(tm, 2)
-    x = x_hi * 2 + lo
-
-    def dev(xx=x, yy=y, zz=z, cc=core):
-        return (lax.div(xx, 2) * 2 + cc, zz * 8 + yy * 2 + lax.rem(xx, 2))
-
-    def ring(value, step):
-        return lax.rem(value + step, 4)
-
-    mate = x_hi * 2 + 1 - lo
-    here = {"x": x, "y": y, "z": z}
-    index = {axis: [ring(here[axis], d) for d in range(4)] for axis in "xyz"}
-    hop = {axis: [dev(**{axis * 2: index[axis][d]}) for d in range(4)] for axis in "xyz"}
-
-    count = [0, 0]
-    sends = []
-
-    def settle():
-        for copy in sends:
-            copy.wait_send()
-        sends.clear()
-
-    def local(src, dst):
-        i = count[0]
-        count[0] += 1
-        copy = pltpu.make_async_copy(src, dst, local_sem.at[i])
-        copy.start()
-        return copy
-
-    def send(src, dst, to):
-        i = count[1]
-        count[1] += 1
-        copy = pltpu.make_async_remote_copy(
-            src_ref=src, dst_ref=dst, send_sem=send_sem.at[i], recv_sem=recv_sem.at[i],
-            device_id=to, device_id_type=MESH,
-        )
-        copy.start()
-        sends.append(copy)
-        return copy
-
+    here = Place(local_sem, send_sem, recv_sem)
+    core, x, y, z, lo = here.core, here.x, here.y, here.z, here.lo
+    hop, local, send = here.hop, here.local, here.send
     la, lb = pl.ds(0, XL), pl.ds(XL, YL)
     ids_in = local(shots_in, ids_v)
     width_in = local(band_in, band_s)
     feat_a = local(feat.at[:, :, la], fv.at[:, :, la])
     feat_b = local(feat.at[:, :, lb], fv.at[:, :, lb])
 
-    barrier = pltpu.get_barrier_semaphore()
-    friends = [hop[axis][d] for axis in "xyz" for d in (1, 2, 3)] + [dev(cc=1 - core)]
-    for friend in friends:
-        pl.semaphore_signal(barrier, inc=1, device_id=friend, device_id_type=MESH)
-
-    def iota(shape, axis):
-        return lax.broadcasted_iota(jnp.int32, shape, axis)
+    everybody = here.greet([hop["y"][1], hop["y"][3], here.mate])
 
     frame, other = iota((BLOCK, 128), 0), iota((BLOCK, 128), 1)
     distance = jnp.abs(frame - other)
@@ -137,11 +147,11 @@
                 part[r // 2, r % 2, 32 * c : 32 * c + size, lanes] = got[32 * r : 32 * r + size].astype(BF16)
 
     l1, l2 = pl.ds(0, XL // 2), pl.ds(XL // 2, XL // 2)
-    up, down, side, twin = hop["y"][1], hop["y"][3], dev(xx=mate), dev(cc=1 - core)
+    up, down, side = hop["y"][1], hop["y"][3], here.mate
 
     feat_a.wait()
     partial_sums(slice(0, XL))
-    pl.semaphore_wait(barrier, len(friends))
+    everybody()
     x_first = {dy: send(part.at[dy, 1, :, la], xa.at[dy], side) for dy in (2, 1, 3, 0)}
     feat_b.wait()
     partial_sums(slice(XL, D))
@@ -228,9 +238,24 @@
         part[0, 0, :, XL:D].astype(F32) + ynu[0].astype(F32) + ynd[0].astype(F32) + yx[...].astype(F32),
         slice(XL, D),
     )
-    pooled_twin = send(pb.at[pl.ds(0, PADDED)], pb.at[pl.ds(PADDED, PADDED)], twin)
-
-    grad_twin = []
+    for copy in wgt_in:
+        copy.wait()
+    here.settle()
+
+
+def main_kernel(
+    pooled, wv, cv, sel,
+    out_proj, out_grad,
+    pa, pre, pb, pt, gr, g,
+    fu, fd, nu, nd, r1, fu2, fd2, nu2, nd2, r2, r3,
+    send_sem, recv_sem,
+):
+    here = Place(None, send_sem, recv_sem)
+    index, hop, send, settle, twin = here.index, here.hop, here.send, here.settle, here.twin
+    everybody = here.greet([hop[a][d] for a in "xyz" for d in (1, 2, 3)] + [twin])
+    pb[0:PADDED, :] = pooled[...]
+
+    grad_twin, pooled_twin = [], []
 
     def gelu_rows(values, cotangent):
         square = values * values
@@ -240,8 +265,7 @@
         return (values * plus).astype(BF16), (cotangent * slope).astype(BF16)
 
     def forward(j):
-        wgt_in[j].wait()
-        pre[...] = jnp.dot(pb[0:PADDED, :], wv[j], preferred_element_type=F32)
+        pre[...] = jnp.dot(pooled[...], wv[j], preferred_element_type=F32)
 
         @pl.loop(0, 11)
         def _(i):
@@ -250,15 +274,18 @@
             pa[j, rows, :] = act
             gr[j, rows, :] = grad
 
+        if j == 0:
+            everybody()
+            pooled_twin.append(send(pb.at[pl.ds(0, PADDED)], pb.at[pl.ds(PADDED, PADDED)], twin))
         grad_twin.append(send(gr.at[j, pl.ds(0, PADDED)], gr.at[j, pl.ds(PADDED, PADDED)], twin))
 
     def give(j):
         @pl.loop(0, 10)
         def _(i):
             rows = pl.ds(pl.multiple_of(i * 16, 16), 16)
-            out_proj[pl.ds(i * 8, 8), :, columns[j]] = pa[j, rows, :].reshape(8, 2, CHUNK)
-
-        out_proj[80, :, columns[j]] = pa[j, 160:162, :]
+            out_proj[pl.ds(i * 8, 8), :, pl.ds(j * CHUNK, CHUNK)] = pa[j, rows, :].reshape(8, 2, CHUNK)
+
+        out_proj[80, :, pl.ds(j * CHUNK, CHUNK)] = pa[j, 160:162, :]
 
     msg = {}
 
@@ -348,7 +375,7 @@
                 out_grad[S3 * s : S3 * s + S3, base : base + CHUNK] = total
 
     forward(0)
-    pooled_twin.wait_recv()
+    pooled_twin[0].wait_recv()
     pt[...] = lax.dot_general(
         sel[...], pb[...], (((1,), (1,)), ((), ())), preferred_element_type=F32
     ).astype(BF16)
@@ -394,51 +421,51 @@
         copy.wait()
 
 
-N_LOCAL = 4 + 4 + 4
-N_SEND = 160
-
-
 def per_device(features, shot_ids, band_width, proj_weight, cotangent):
     frames = jnp.swapaxes(features, 1, 2).reshape(2, TOKS * POOL, D)
     cot = cotangent.transpose(1, 2, 0, 3).reshape(TOKS, 2, H)
     vm = lambda *shape: pltpu.VMEM(shape, BF16)
-    scratch = [
-        vm(2, TOKS * POOL, D), vm(4, D, CHUNK), vm(4, TOKS, 2, CHUNK), vm(4, PADDED, CHUNK),
-        vm(4, PADDED, CHUNK),
-        pltpu.VMEM((PADDED, CHUNK), F32), vm(256, 256), vm(4, 2, ROWS, D), vm(576, D),
-        vm(2 * PADDED, D), vm(576, 2 * PADDED), vm(4, 2 * PADDED, CHUNK),
-        vm(4, ROWS, XL), vm(ROWS, XL // 2), vm(ROWS, XL // 2), vm(ROWS, XL), vm(ROWS, XL),
-        vm(ROWS, YL), vm(ROWS, YL), vm(2, ROWS, YL), vm(2, ROWS, YL), vm(ROWS, YL), vm(ROWS, YL),
-        vm(3, 4, 2, 4, S1, CHUNK),
-        vm(3, 4, S1, CHUNK), vm(3, 4, S1, CHUNK), vm(3, 4, 2, S1, CHUNK), vm(3, 4, 2, S1, CHUNK),
-        vm(3, 4, 4, S2, CHUNK), vm(3, 2, S2, CHUNK), vm(3, 2, S2, CHUNK),
-        vm(3, 2, 2, S2, CHUNK), vm(3, 2, 2, S2, CHUNK),
-        vm(3, 4, 2, 2, S3, CHUNK), vm(3, 4, 2, 2, S3, CHUNK),
-        pltpu.VMEM(shot_ids.shape, jnp.int32), pltpu.SMEM(band_width.shape, jnp.int32),
-        pltpu.SemaphoreType.DMA((N_LOCAL,)),
-        pltpu.SemaphoreType.DMA((N_SEND,)),
-        pltpu.SemaphoreType.DMA((N_SEND,)),
-    ]
+    sems = lambda n: pltpu.SemaphoreType.DMA((n,))
     any_spec = pl.BlockSpec(memory_space=pl.ANY)
     vmem_spec = pl.BlockSpec(memory_space=pltpu.VMEM)
-    inputs = [
-        pltpu.with_memory_space_constraint(a, pltpu.HBM)
-        for a in (frames, proj_weight, cot, shot_ids, band_width)
-    ]
+    pin = lambda space, *arrays: [pltpu.with_memory_space_constraint(a, space) for a in arrays]
+    shared = pl.pallas_call(
+        pool_kernel,
+        out_shape=(vm(PADDED, D), vm(4, D, CHUNK), vm(4, PADDED, CHUNK), vm(576, D)),
+        in_specs=[any_spec] * 5,
+        out_specs=(vmem_spec,) * 4,
+        scratch_shapes=[
+            vm(2, TOKS * POOL, D), vm(4, TOKS, 2, CHUNK), vm(256, 256), vm(4, 2, ROWS, D),
+            vm(4, ROWS, XL), vm(ROWS, XL // 2), vm(ROWS, XL // 2), vm(ROWS, XL), vm(ROWS, XL),
+            vm(ROWS, YL), vm(ROWS, YL), vm(2, ROWS, YL), vm(2, ROWS, YL), vm(ROWS, YL), vm(ROWS, YL),
+            pltpu.VMEM(shot_ids.shape, jnp.int32), pltpu.SMEM(band_width.shape, jnp.int32),
+            sems(12), sems(24), sems(24),
+        ],
+        compiler_params=pltpu.CompilerParams(
+            collective_id=0, has_side_effects=True, vmem_limit_bytes=24 * 1024 * 1024
+        ),
+        cost_estimate=pl.CostEstimate(flops=10**9, bytes_accessed=14 * 10**6, transcendentals=0),
+    )(*pin(pltpu.HBM, frames, proj_weight, cot, shot_ids, band_width))
     projected, weight_grad = pl.pallas_call(
-        kernel,
-        out_shape=(
-            pltpu.VMEM(cot.shape, BF16),
-            pltpu.VMEM((9, H), F32),
+        main_kernel,
+        out_shape=(pltpu.VMEM(cot.shape, BF16), pltpu.VMEM((9, H), F32)),
+        in_specs=[vmem_spec] * 4,
+        out_specs=(vmem_spec, vmem_spec),
+        scratch_shapes=[
+            vm(4, PADDED, CHUNK), pltpu.VMEM((PADDED, CHUNK), F32),
+            vm(2 * PADDED, D), vm(576, 2 * PADDED), vm(4, 2 * PADDED, CHUNK),
+            vm(3, 4, 2, 4, S1, CHUNK),
+            vm(3, 4, S1, CHUNK), vm(3, 4, S1, CHUNK), vm(3, 4, 2, S1, CHUNK), vm(3, 4, 2, S1, CHUNK),
+            vm(3, 4, 4, S2, CHUNK), vm(3, 2, S2, CHUNK), vm(3, 2, S2, CHUNK),
+            vm(3, 2, 2, S2, CHUNK), vm(3, 2, 2, S2, CHUNK),
+            vm(3, 4, 2, 2, S3, CHUNK), vm(3, 4, 2, 2, S3, CHUNK),
+            sems(144), sems(144),
+        ],
+        compiler_params=pltpu.CompilerParams(
+            collective_id=1, has_side_effects=True, vmem_limit_bytes=36 * 1024 * 1024
         ),
-        in_specs=[any_spec] * 5,
-        out_specs=(vmem_spec, vmem_spec),
-        scratch_shapes=scratch,
-        compiler_params=pltpu.CompilerParams(
-            collective_id=0, has_side_effects=True, vmem_limit_bytes=50 * 1024 * 1024
-        ),
-        cost_estimate=pl.CostEstimate(flops=4 * 10**9, bytes_accessed=14 * 10**6, transcendentals=600000),
-    )(*inputs)
+        cost_estimate=pl.CostEstimate(flops=3 * 10**9, bytes_accessed=10**6, transcendentals=600000),
+    )(*pin(pltpu.VMEM, *shared))
     projected, weight_grad = pl.pallas_call(
         hand_over,
         out_shape=(
@@ -448,7 +475,7 @@
         in_specs=[vmem_spec, vmem_spec],
         out_specs=(any_spec, any_spec),
         scratch_shapes=[pltpu.SemaphoreType.DMA((10,))],
-    )(*(pltpu.with_memory_space_constraint(a, pltpu.VMEM) for a in (projected, weight_grad)))
+    )(*pin(pltpu.VMEM, projected, weight_grad))
     return projected.reshape(1, TOKS, 2, H).transpose(2, 0, 1, 3), weight_grad
 
 

time: 66.7 us -> 69 us (1.034)
  Pallas kernels: 65.9 us -> 68 us
    pallas_call x1 -> x2, Pallas kernels: 64.7 us -> 66.9 us  [the longest x1 40.2 us: per_device(): pl.pallas_call(main_kernel, out_shape=(pltpu.VMEM(cot.shape, BF16), pltpu...]
where the time goes in v3:
time: 69 us; the launch traced here: 68.8 us
  Pallas kernels  68 us (99%)
  between operations  0.81 us (1%)
    pallas_call x1, Pallas kernels, per_device(): pl.pallas_call(main_kernel, out_shape=(pltpu.VMEM(cot.shape, BF16), pltpu...  40.2 us
    pallas_call x1, Pallas kernels, per_device(): pl.pallas_call(pool_kernel, out_shape=(vm(PADDED, D), vm(4, D, CHUNK), vm...  26.7 us

profile of v3, /device:TPU:0, one launch (start us, length us, event | category | flops | bytes accessed | tf_op | source)
XLA Modules:
  0.0 68.8 jit_solution(14172480857990956245)
XLA Ops:
  0.6 26.7 %shard_map.68 = (bf16[176,1152]{1,0:T(8,128)(2,1)S(1)}, bf16[4,1152,896]{2,1,0:T(8,128)(2,1)S(1)}, bf16[4,176,896]{2,1,0:T(8,128)(2,1)S(1)}, bf16[576,1152]{1,0:T(8,128)(2,1)S(1)}) custom-call(bf16[2,648,1152]{2,1,0:T(8,128)(2,1)} %bitcast.9, bf16[1152,3584]{1,0:T(8,128)(2,1)} %wgt.1, bf16[81,2,3584]{2,1,0:T(2,128)(2,1)} %bitcast.10, s32[2,256]{1,0:T(2,128)} %shots_in.1, ...), custom_call_target="tpu_custom_call" | custom-call | flops 1000000000 | bytes 14000000 | tf_op jit(solution)/shard_map/pallas_call | solution.py:432
  27.3 40.2 %shard_map.69 = (bf16[81,2,3584]{2,1,0:T(2,128)(2,1)S(1)}, f32[9,3584]{1,0:T(8,128)S(1)}) custom-call(bf16[176,1152]{1,0:T(8,128)(2,1)S(1)} %get-tuple-element.10.pooled, bf16[4,1152,896]{2,1,0:T(8,128)(2,1)S(1)} %get-tuple-element.11.wv, bf16[4,176,896]{2,1,0:T(8,128)(2,1)S(1)} %get-tuple-element.12.cv, bf16[576,1152]{1,0:T(8,128)(2,1)S(1)} %get-tuple-element.13.sel), custom_call_target="tpu_custom_call" | custom-call | flops 3000000000 | bytes 1000000 | tf_op jit(solution)/shard_map/pallas_call | solution.py:449
  67.5 1.2 %shard_map.70 = (bf16[81,2,3584]{2,1,0:T(2,128)(2,1)}, f32[9,3584]{1,0:T(8,128)}) custom-call(bf16[81,2,3584]{2,1,0:T(2,128)(2,1)S(1)} %get-tuple-element.14.projected, f32[9,3584]{1,0:T(8,128)S(1)} %get-tuple-element.15.weight_grad), custom_call_target="tpu_custom_call" | custom-call | tf_op jit(solution)/shard_map/pallas_call | solution.py:469

commit v4 on v3

--- a/solution.py
+++ b/solution.py
@@ -18,6 +18,7 @@
 YL = D - XL
 CHUNK = H // 4
 ORDER = (("z", "y", "x"), ("y", "x", "z"), ("x", "z", "y"))
+SLOTS = ((2, 0), (1, 1), (2, 1), (3, 0), (1, 0), (3, 1), (0, 0), (0, 1))
 S1, S2, S3 = 24, 12, 3
 C0 = 0.7978845608028654
 C1 = 0.044715
@@ -165,14 +166,19 @@
     wgt_in = [local(wgt.at[:, columns[j]], wv.at[j]) for j in range(4)]
 
     row, lane = iota((576, 128), 0), iota((576, 128), 1)
-    which = lax.div(row, 192)
-    first, second, third = lax.div(lax.rem(row, 192), 48), lax.div(lax.rem(row, 48), 12), lax.div(lax.rem(row, 12), 3)
+    which, slot = lax.div(row, 192), lax.div(lax.rem(row, 192), S1)
+    half, first = jnp.zeros_like(row), jnp.zeros_like(row)
+    for p, (d, h) in enumerate(SLOTS):
+        first = jnp.where(slot == p, d, first)
+        half = jnp.where(slot == p, h, half)
+    second = half * 2 + lax.div(lax.rem(row, S1), S2)
+    third = lax.div(lax.rem(row, S2), S3)
     at = {}
-    for axis in "xyz":
-        at[axis] = jnp.zeros((576, 128), jnp.int32)
-        for s in range(3):
-            place = (first, second, third)[ORDER[s].index(axis)]
-            at[axis] = jnp.where(which == s, place, at[axis])
+    for axis, mine in (("x", x), ("y", y), ("z", z)):
+        far = jnp.zeros_like(row)
+        for s in range(3):
+            far = jnp.where(which == s, (first, second, third)[ORDER[s].index(axis)], far)
+        at[axis] = lax.rem(far + mine, 4)
     owner = (lax.div(at["x"], 2) * 2 + core) * 32 + at["z"] * 8 + at["y"] * 2 + lax.rem(at["x"], 2)
     wanted = owner * 9 + which * S3 + lax.rem(row, S3)
     for k in range(D // 128):
@@ -247,11 +253,11 @@
     pooled, wv, cv, sel,
     out_proj, out_grad,
     pa, pre, pb, pt, gr, g,
-    fu, fd, nu, nd, r1, fu2, fd2, nu2, nd2, r2, r3,
+    ru, rd, nu, nd, r1, ru2, rd2, nu2, nd2, r2, r3,
     send_sem, recv_sem,
 ):
     here = Place(None, send_sem, recv_sem)
-    index, hop, send, settle, twin = here.index, here.hop, here.send, here.settle, here.twin
+    hop, send, settle, twin = here.hop, here.send, here.settle, here.twin
     everybody = here.greet([hop[a][d] for a in "xyz" for d in (1, 2, 3)] + [twin])
     pb[0:PADDED, :] = pooled[...]
 
@@ -300,79 +306,74 @@
         grad_twin[j].wait_recv()
         got = jnp.dot(pt[...], gr[j], preferred_element_type=F32)
         for s in range(3):
-            for a in range(4):
-                for h in range(2):
-                    base = s * 192 + a * 48 + h * S1
-                    g[s, a, h, j] = got[base : base + S1].astype(BF16)
-        for s in range(3):
-            i, to = index[ORDER[s][0]], hop[ORDER[s][0]]
-            msg["fu", s, j] = send(g.at[s, i[2], 0, j], fu.at[s, j], to[1])
-            msg["fd", s, j] = send(g.at[s, i[2], 1, j], fd.at[s, j], to[3])
-        for s in range(3):
-            i, to = index[ORDER[s][0]], hop[ORDER[s][0]]
-            msg["nu1", s, j] = send(g.at[s, i[1], 1, j], nu.at[s, j, 1], to[1])
-            msg["nd0", s, j] = send(g.at[s, i[3], 0, j], nd.at[s, j, 0], to[3])
+            for p in range(8):
+                base = s * 192 + p * S1
+                g[s, j, p] = got[base : base + S1].astype(BF16)
+        for s in range(3):
+            to = hop[ORDER[s][0]]
+            msg["ru", s, j] = send(g.at[s, j, pl.ds(0, 2)], ru.at[s, j], to[1])
+            msg["rd", s, j] = send(g.at[s, j, pl.ds(2, 2)], rd.at[s, j], to[3])
 
     def relay(j):
         for s in range(3):
-            i, to = index[ORDER[s][0]], hop[ORDER[s][0]]
-            wait(("fu", s, j))
-            fu[s, j] = add16(fu[s, j], g[s, i[1], 0, j])
-            msg["nu0", s, j] = send(fu.at[s, j], nu.at[s, j, 0], to[1])
-            wait(("fd", s, j))
-            fd[s, j] = add16(fd[s, j], g[s, i[3], 1, j])
-            msg["nd1", s, j] = send(fd.at[s, j], nd.at[s, j, 1], to[3])
+            to = hop[ORDER[s][0]]
+            wait(("ru", s, j))
+            ru[s, j, 0] = add16(ru[s, j, 0], g[s, j, 4])
+            msg["nu", s, j] = send(ru.at[s, j, 0], nu.at[s, j], to[1])
+            wait(("rd", s, j))
+            rd[s, j, 0] = add16(rd[s, j, 0], g[s, j, 5])
+            msg["nd", s, j] = send(rd.at[s, j, 0], nd.at[s, j], to[3])
 
     def finish(j):
-        for s in range(3):
-            i = index[ORDER[s][0]]
-            wait(("nu1", s, j), ("nd0", s, j), ("nu0", s, j), ("nd1", s, j))
-            value = add3(g[s, i[0], :, j], nu[s, j], nd[s, j]).reshape(2 * S1, CHUNK)
-            for b in range(4):
-                r1[s, b, j] = value[S2 * b : S2 * b + S2].astype(BF16)
+        q, k = j // 2, j % 2
+        for s in range(3):
+            wait(("nu", s, j), ("nd", s, j))
+            for h, value in enumerate(
+                (add3(g[s, j, 6], nu[s, j], rd[s, j, 1]), add3(g[s, j, 7], ru[s, j, 1], nd[s, j]))
+            ):
+                for b in range(2):
+                    slot = SLOTS.index((2 * h + b, k))
+                    r1[s, q, slot] = value[S2 * b : S2 * b + S2].astype(BF16)
 
     def second_stage(q):
         for s in range(3):
-            i, to = index[ORDER[s][1]], hop[ORDER[s][1]]
-            msg["fu2", s, q] = send(r1.at[s, i[2], 2 * q], fu2.at[s, q], to[1])
-            msg["fd2", s, q] = send(r1.at[s, i[2], 2 * q + 1], fd2.at[s, q], to[3])
-        for s in range(3):
-            i, to = index[ORDER[s][1]], hop[ORDER[s][1]]
-            msg["mu1", s, q] = send(r1.at[s, i[1], 2 * q + 1], nu2.at[s, q, 1], to[1])
-            msg["md0", s, q] = send(r1.at[s, i[3], 2 * q], nd2.at[s, q, 0], to[3])
+            to = hop[ORDER[s][1]]
+            msg["ru2", s, q] = send(r1.at[s, q, pl.ds(0, 2)], ru2.at[s, q], to[1])
+            msg["rd2", s, q] = send(r1.at[s, q, pl.ds(2, 2)], rd2.at[s, q], to[3])
 
     def second_relay(q):
         for s in range(3):
-            i, to = index[ORDER[s][1]], hop[ORDER[s][1]]
-            wait(("fu2", s, q))
-            fu2[s, q] = add16(fu2[s, q], r1[s, i[1], 2 * q])
-            msg["mu0", s, q] = send(fu2.at[s, q], nu2.at[s, q, 0], to[1])
-            wait(("fd2", s, q))
-            fd2[s, q] = add16(fd2[s, q], r1[s, i[3], 2 * q + 1])
-            msg["md1", s, q] = send(fd2.at[s, q], nd2.at[s, q, 1], to[3])
-
-    def third_stage(q):
-        for s in range(3):
-            i = index[ORDER[s][1]]
-            wait(("mu1", s, q), ("md0", s, q), ("mu0", s, q), ("md1", s, q))
-            for k in range(2):
-                value = add3(r1[s, i[0], 2 * q + k], nu2[s, q, k], nd2[s, q, k])
+            to = hop[ORDER[s][1]]
+            wait(("ru2", s, q))
+            ru2[s, q, 0] = add16(ru2[s, q, 0], r1[s, q, 4])
+            msg["nu2", s, q] = send(ru2.at[s, q, 0], nu2.at[s, q], to[1])
+            wait(("rd2", s, q))
+            rd2[s, q, 0] = add16(rd2[s, q, 0], r1[s, q, 5])
+            msg["nd2", s, q] = send(rd2.at[s, q, 0], nd2.at[s, q], to[3])
+
+    def second_finish(q):
+        for s in range(3):
+            wait(("nu2", s, q), ("nd2", s, q))
+            for k, value in enumerate(
+                (add3(r1[s, q, 6], nu2[s, q], rd2[s, q, 1]), add3(r1[s, q, 7], ru2[s, q, 1], nd2[s, q]))
+            ):
                 for c in range(4):
-                    r2[s, c, q, k] = value[S3 * c : S3 * c + S3].astype(BF16)
-            i, to = index[ORDER[s][2]], hop[ORDER[s][2]]
+                    r2[s, c, 2 * q + k] = value[S3 * c : S3 * c + S3].astype(BF16)
+
+    def third_stage():
+        for s in range(3):
+            to = hop[ORDER[s][2]]
             for d in (2, 1, 3):
-                msg["last", s, q, d] = send(r2.at[s, i[d], q], r3.at[s, d, q], to[d])
-
-    def owned(q):
-        for s in range(3):
-            i = index[ORDER[s][2]]
-            wait(*(("last", s, q, d) for d in (1, 2, 3)))
-            for k in range(2):
-                total = r2[s, i[0], q, k].astype(F32)
+                msg["last", s, d] = send(r2.at[s, d], r3.at[s, d], to[d])
+
+    def owned():
+        for s in range(3):
+            wait(*(("last", s, d) for d in (1, 2, 3)))
+            for j in range(4):
+                total = r2[s, 0, j].astype(F32)
                 for d in (1, 2, 3):
-                    total = total + r3[s, d, q, k].astype(F32)
-                base = (2 * q + k) * CHUNK
-                out_grad[S3 * s : S3 * s + S3, base : base + CHUNK] = total
+                    total = total + r3[s, d, j].astype(F32)
+                out_grad[S3 * s : S3 * s + S3, j * CHUNK : j * CHUNK + CHUNK] = total
 
     forward(0)
     pooled_twin[0].wait_recv()
@@ -390,23 +391,23 @@
     backward(3)
     relay(2)
     finish(0)
-    relay(3)
     finish(1)
     second_stage(0)
+    relay(3)
     give(0)
     finish(2)
     second_relay(0)
     finish(3)
     second_stage(1)
     give(1)
-    third_stage(0)
+    second_finish(0)
     give(2)
     second_relay(1)
     give(3)
     settle()
-    third_stage(1)
-    owned(0)
-    owned(1)
+    second_finish(1)
+    third_stage()
+    owned()
     settle()
 
 
@@ -454,12 +455,12 @@
         scratch_shapes=[
             vm(4, PADDED, CHUNK), pltpu.VMEM((PADDED, CHUNK), F32),
             vm(2 * PADDED, D), vm(576, 2 * PADDED), vm(4, 2 * PADDED, CHUNK),
-            vm(3, 4, 2, 4, S1, CHUNK),
-            vm(3, 4, S1, CHUNK), vm(3, 4, S1, CHUNK), vm(3, 4, 2, S1, CHUNK), vm(3, 4, 2, S1, CHUNK),
-            vm(3, 4, 4, S2, CHUNK), vm(3, 2, S2, CHUNK), vm(3, 2, S2, CHUNK),
-            vm(3, 2, 2, S2, CHUNK), vm(3, 2, 2, S2, CHUNK),
-            vm(3, 4, 2, 2, S3, CHUNK), vm(3, 4, 2, 2, S3, CHUNK),
-            sems(144), sems(144),
+            vm(3, 4, 8, S1, CHUNK),
+            vm(3, 4, 2, S1, CHUNK), vm(3, 4, 2, S1, CHUNK), vm(3, 4, S1, CHUNK), vm(3, 4, S1, CHUNK),
+            vm(3, 2, 8, S2, CHUNK), vm(3, 2, 2, S2, CHUNK), vm(3, 2, 2, S2, CHUNK),
+            vm(3, 2, S2, CHUNK), vm(3, 2, S2, CHUNK),
+            vm(3, 4, 4, S3, CHUNK), vm(3, 4, 4, S3, CHUNK),
+            sems(88), sems(88),
         ],
         compiler_params=pltpu.CompilerParams(
             collective_id=1, has_side_effects=True, vmem_limit_bytes=36 * 1024 * 1024

time: 69 us -> 69.1 us (level)
  no operation moved by 1% of the time
where the time goes in v4:
time: 69.1 us; the launch traced here: 68.9 us
  Pallas kernels  68.1 us (99%)
  between operations  0.81 us (1%)
    pallas_call x1, Pallas kernels, per_device(): pl.pallas_call(main_kernel, out_shape=(pltpu.VMEM(cot.shape, BF16), pltpu...  40.3 us
    pallas_call x1, Pallas kernels, per_device(): pl.pallas_call(pool_kernel, out_shape=(vm(PADDED, D), vm(4, D, CHUNK), vm...  26.7 us

profile of v4, /device:TPU:0, one launch (start us, length us, event | category | flops | bytes accessed | tf_op | source)
XLA Modules:
  0.0 68.9 jit_solution(17757041084384588006)
XLA Ops:
  0.6 26.7 %shard_map.68 = (bf16[176,1152]{1,0:T(8,128)(2,1)S(1)}, bf16[4,1152,896]{2,1,0:T(8,128)(2,1)S(1)}, bf16[4,176,896]{2,1,0:T(8,128)(2,1)S(1)}, bf16[576,1152]{1,0:T(8,128)(2,1)S(1)}) custom-call(bf16[2,648,1152]{2,1,0:T(8,128)(2,1)} %bitcast.9, bf16[1152,3584]{1,0:T(8,128)(2,1)} %wgt.1, bf16[81,2,3584]{2,1,0:T(2,128)(2,1)} %bitcast.10, s32[2,256]{1,0:T(2,128)} %shots_in.1, ...), custom_call_target="tpu_custom_call" | custom-call | flops 1000000000 | bytes 14000000 | tf_op jit(solution)/shard_map/pallas_call | solution.py:433
  27.3 40.3 %shard_map.69 = (bf16[81,2,3584]{2,1,0:T(2,128)(2,1)S(1)}, f32[9,3584]{1,0:T(8,128)S(1)}) custom-call(bf16[176,1152]{1,0:T(8,128)(2,1)S(1)} %get-tuple-element.10.pooled, bf16[4,1152,896]{2,1,0:T(8,128)(2,1)S(1)} %get-tuple-element.11.wv, bf16[4,176,896]{2,1,0:T(8,128)(2,1)S(1)} %get-tuple-element.12.cv, bf16[576,1152]{1,0:T(8,128)(2,1)S(1)} %get-tuple-element.13.sel), custom_call_target="tpu_custom_call" | custom-call | flops 3000000000 | bytes 1000000 | tf_op jit(solution)/shard_map/pallas_call | solution.py:450
  67.6 1.2 %shard_map.70 = (bf16[81,2,3584]{2,1,0:T(2,128)(2,1)}, f32[9,3584]{1,0:T(8,128)}) custom-call(bf16[81,2,3584]{2,1,0:T(2,128)(2,1)S(1)} %get-tuple-element.14.projected, f32[9,3584]{1,0:T(8,128)S(1)} %get-tuple-element.15.weight_grad), custom_call_target="tpu_custom_call" | custom-call | tf_op jit(solution)/shard_map/pallas_call | solution.py:470

commit v5 on v4

--- a/solution.py
+++ b/solution.py
@@ -16,7 +16,10 @@
 PADDED = 176
 XL = 512
 YL = D - XL
-CHUNK = H // 4
+CHUNK = 512
+STEPS = H // CHUNK
+HALF = CHUNK // 2
+GROUPS = ((0, 3), (3, 6), (6, 7))
 ORDER = (("z", "y", "x"), ("y", "x", "z"), ("x", "z", "y"))
 SLOTS = ((2, 0), (1, 1), (2, 1), (3, 0), (1, 0), (3, 1), (0, 0), (0, 1))
 S1, S2, S3 = 24, 12, 3
@@ -161,9 +164,9 @@
     near_up = {1: send(part.at[1, 1, :, lb], ynu.at[1], up)}
     near_down = {0: send(part.at[3, 0, :, lb], ynd.at[0], down)}
 
-    columns = [pl.ds(j * CHUNK, CHUNK) for j in range(4)]
-    cot_in = [local(cot.at[:, :, columns[j]], cn.at[j]) for j in range(4)]
-    wgt_in = [local(wgt.at[:, columns[j]], wv.at[j]) for j in range(4)]
+    columns = [pl.ds(j * CHUNK, CHUNK) for j in range(STEPS)]
+    cot_in = [local(cot.at[:, :, columns[j]], cn.at[j]) for j in range(STEPS)]
+    wgt_in = [local(wgt.at[:, columns[j]], wv.at[j]) for j in range(STEPS)]
 
     row, lane = iota((576, 128), 0), iota((576, 128), 1)
     which, slot = lax.div(row, 192), lax.div(lax.rem(row, 192), S1)
@@ -202,7 +205,7 @@
     take(3)
     near_down2 = [send(xa.at[3, :, l1], xnd.at[:, l1], down)]
 
-    for j in range(4):
+    for j in range(STEPS):
         cot_in[j].wait()
 
         @pl.loop(0, 10)
@@ -325,40 +328,43 @@
             msg["nd", s, j] = send(rd.at[s, j, 0], nd.at[s, j], to[3])
 
     def finish(j):
-        q, k = j // 2, j % 2
         for s in range(3):
             wait(("nu", s, j), ("nd", s, j))
             for h, value in enumerate(
                 (add3(g[s, j, 6], nu[s, j], rd[s, j, 1]), add3(g[s, j, 7], ru[s, j, 1], nd[s, j]))
             ):
                 for b in range(2):
-                    slot = SLOTS.index((2 * h + b, k))
-                    r1[s, q, slot] = value[S2 * b : S2 * b + S2].astype(BF16)
+                    rows = value[S2 * b : S2 * b + S2].astype(BF16)
+                    for k in range(2):
+                        r1[s, SLOTS.index((2 * h + b, k)), j] = rows[:, HALF * k : HALF * k + HALF]
 
     def second_stage(q):
+        steps = pl.ds(GROUPS[q][0], GROUPS[q][1] - GROUPS[q][0])
         for s in range(3):
             to = hop[ORDER[s][1]]
-            msg["ru2", s, q] = send(r1.at[s, q, pl.ds(0, 2)], ru2.at[s, q], to[1])
-            msg["rd2", s, q] = send(r1.at[s, q, pl.ds(2, 2)], rd2.at[s, q], to[3])
+            msg["ru2", s, q] = send(r1.at[s, pl.ds(0, 2), steps], ru2.at[s, :, steps], to[1])
+            msg["rd2", s, q] = send(r1.at[s, pl.ds(2, 2), steps], rd2.at[s, :, steps], to[3])
 
     def second_relay(q):
+        steps = pl.ds(GROUPS[q][0], GROUPS[q][1] - GROUPS[q][0])
         for s in range(3):
             to = hop[ORDER[s][1]]
             wait(("ru2", s, q))
-            ru2[s, q, 0] = add16(ru2[s, q, 0], r1[s, q, 4])
-            msg["nu2", s, q] = send(ru2.at[s, q, 0], nu2.at[s, q], to[1])
+            ru2[s, 0, steps] = add16(ru2[s, 0, steps], r1[s, 4, steps])
+            msg["nu2", s, q] = send(ru2.at[s, 0, steps], nu2.at[s, steps], to[1])
             wait(("rd2", s, q))
-            rd2[s, q, 0] = add16(rd2[s, q, 0], r1[s, q, 5])
-            msg["nd2", s, q] = send(rd2.at[s, q, 0], nd2.at[s, q], to[3])
+            rd2[s, 0, steps] = add16(rd2[s, 0, steps], r1[s, 5, steps])
+            msg["nd2", s, q] = send(rd2.at[s, 0, steps], nd2.at[s, steps], to[3])
 
     def second_finish(q):
         for s in range(3):
             wait(("nu2", s, q), ("nd2", s, q))
-            for k, value in enumerate(
-                (add3(r1[s, q, 6], nu2[s, q], rd2[s, q, 1]), add3(r1[s, q, 7], ru2[s, q, 1], nd2[s, q]))
-            ):
-                for c in range(4):
-                    r2[s, c, 2 * q + k] = value[S3 * c : S3 * c + S3].astype(BF16)
+            for j in range(*GROUPS[q]):
+                for k, value in enumerate(
+                    (add3(r1[s, 6, j], nu2[s, j], rd2[s, 1, j]), add3(r1[s, 7, j], ru2[s, 1, j], nd2[s, j]))
+                ):
+                    for c in range(4):
+                        r2[s, c, j, :, HALF * k : HALF * k + HALF] = value[S3 * c : S3 * c + S3].astype(BF16)
 
     def third_stage():
         for s in range(3):
@@ -369,7 +375,7 @@
     def owned():
         for s in range(3):
             wait(*(("last", s, d) for d in (1, 2, 3)))
-            for j in range(4):
+            for j in range(STEPS):
                 total = r2[s, 0, j].astype(F32)
                 for d in (1, 2, 3):
                     total = total + r3[s, d, j].astype(F32)
@@ -388,25 +394,43 @@
     forward(3)
     backward(2)
     relay(1)
+    forward(4)
     backward(3)
     relay(2)
     finish(0)
+    forward(5)
+    backward(4)
+    relay(3)
     finish(1)
+    forward(6)
+    backward(5)
+    relay(4)
+    finish(2)
     second_stage(0)
-    relay(3)
+    backward(6)
+    relay(5)
+    finish(3)
+    second_relay(0)
+    finish(4)
+    relay(6)
     give(0)
-    finish(2)
-    second_relay(0)
-    finish(3)
+    give(1)
+    finish(5)
     second_stage(1)
-    give(1)
     second_finish(0)
+    finish(6)
+    second_stage(2)
     give(2)
     second_relay(1)
     give(3)
+    second_relay(2)
+    second_finish(1)
+    give(4)
     settle()
-    second_finish(1)
+    second_finish(2)
     third_stage()
+    give(5)
+    give(6)
     owned()
     settle()
 
@@ -432,15 +456,15 @@
     pin = lambda space, *arrays: [pltpu.with_memory_space_constraint(a, space) for a in arrays]
     shared = pl.pallas_call(
         pool_kernel,
-        out_shape=(vm(PADDED, D), vm(4, D, CHUNK), vm(4, PADDED, CHUNK), vm(576, D)),
+        out_shape=(vm(PADDED, D), vm(STEPS, D, CHUNK), vm(STEPS, PADDED, CHUNK), vm(576, D)),
         in_specs=[any_spec] * 5,
         out_specs=(vmem_spec,) * 4,
         scratch_shapes=[
-            vm(2, TOKS * POOL, D), vm(4, TOKS, 2, CHUNK), vm(256, 256), vm(4, 2, ROWS, D),
+            vm(2, TOKS * POOL, D), vm(STEPS, TOKS, 2, CHUNK), vm(256, 256), vm(4, 2, ROWS, D),
             vm(4, ROWS, XL), vm(ROWS, XL // 2), vm(ROWS, XL // 2), vm(ROWS, XL), vm(ROWS, XL),
             vm(ROWS, YL), vm(ROWS, YL), vm(2, ROWS, YL), vm(2, ROWS, YL), vm(ROWS, YL), vm(ROWS, YL),
             pltpu.VMEM(shot_ids.shape, jnp.int32), pltpu.SMEM(band_width.shape, jnp.int32),
-            sems(12), sems(24), sems(24),
+            sems(4 + 2 * STEPS), sems(24), sems(24),
         ],
         compiler_params=pltpu.CompilerParams(
             collective_id=0, has_side_effects=True, vmem_limit_bytes=24 * 1024 * 1024
@@ -453,14 +477,15 @@
         in_specs=[vmem_spec] * 4,
         out_specs=(vmem_spec, vmem_spec),
         scratch_shapes=[
-            vm(4, PADDED, CHUNK), pltpu.VMEM((PADDED, CHUNK), F32),
-            vm(2 * PADDED, D), vm(576, 2 * PADDED), vm(4, 2 * PADDED, CHUNK),
-            vm(3, 4, 8, S1, CHUNK),
-            vm(3, 4, 2, S1, CHUNK), vm(3, 4, 2, S1, CHUNK), vm(3, 4, S1, CHUNK), vm(3, 4, S1, CHUNK),
-            vm(3, 2, 8, S2, CHUNK), vm(3, 2, 2, S2, CHUNK), vm(3, 2, 2, S2, CHUNK),
-            vm(3, 2, S2, CHUNK), vm(3, 2, S2, CHUNK),
-            vm(3, 4, 4, S3, CHUNK), vm(3, 4, 4, S3, CHUNK),
-            sems(88), sems(88),
+            vm(STEPS, PADDED, CHUNK), pltpu.VMEM((PADDED, CHUNK), F32),
+            vm(2 * PADDED, D), vm(576, 2 * PADDED), vm(STEPS, 2 * PADDED, CHUNK),
+            vm(3, STEPS, 8, S1, CHUNK),
+            vm(3, STEPS, 2, S1, CHUNK), vm(3, STEPS, 2, S1, CHUNK),
+            vm(3, STEPS, S1, CHUNK), vm(3, STEPS, S1, CHUNK),
+            vm(3, 8, STEPS, S2, HALF), vm(3, 2, STEPS, S2, HALF), vm(3, 2, STEPS, S2, HALF),
+            vm(3, STEPS, S2, HALF), vm(3, STEPS, S2, HALF),
+            vm(3, 4, STEPS, S3, CHUNK), vm(3, 4, STEPS, S3, CHUNK),
+            sems(144), sems(144),
         ],
         compiler_params=pltpu.CompilerParams(
             collective_id=1, has_side_effects=True, vmem_limit_bytes=36 * 1024 * 1024

time: 69.1 us -> 72.7 us (1.052)
  Pallas kernels: 68.1 us -> 71.9 us
    pallas_call x1, Pallas kernels: 40.3 us -> 44 us  [per_device(): pl.pallas_call(main_kernel, out_shape=(pltpu.VMEM(cot.shape, BF16), pltpu...]
where the time goes in v5:
time: 72.7 us; the launch traced here: 72.6 us
  Pallas kernels  71.9 us (99%)
    pallas_call x1, Pallas kernels, per_device(): pl.pallas_call(main_kernel, out_shape=(pltpu.VMEM(cot.shape, BF16), pltpu...  44 us
    pallas_call x1, Pallas kernels, per_device(): pl.pallas_call(pool_kernel, out_shape=(vm(PADDED, D), vm(STEPS, D, CHUNK)...  26.8 us

profile of v5, /device:TPU:0, one launch (start us, length us, event | category | flops | bytes accessed | tf_op | source)
XLA Modules:
  0.0 72.6 jit_solution(5112855908553363300)
XLA Ops:
  0.6 26.8 %shard_map.68 = (bf16[176,1152]{1,0:T(8,128)(2,1)S(1)}, bf16[7,1152,512]{2,1,0:T(8,128)(2,1)S(1)}, bf16[7,176,512]{2,1,0:T(8,128)(2,1)S(1)}, bf16[576,1152]{1,0:T(8,128)(2,1)S(1)}) custom-call(bf16[2,648,1152]{2,1,0:T(8,128)(2,1)} %bitcast.9, bf16[1152,3584]{1,0:T(8,128)(2,1)} %wgt.1, bf16[81,2,3584]{2,1,0:T(2,128)(2,1)} %bitcast.10, s32[2,256]{1,0:T(2,128)} %shots_in.1, ...), custom_call_target="tpu_custom_call" | custom-call | flops 1000000000 | bytes 14000000 | tf_op jit(solution)/shard_map/pallas_call | solution.py:457
  27.4 44.0 %shard_map.69 = (bf16[81,2,3584]{2,1,0:T(2,128)(2,1)S(1)}, f32[9,3584]{1,0:T(8,128)S(1)}) custom-call(bf16[176,1152]{1,0:T(8,128)(2,1)S(1)} %get-tuple-element.10.pooled, bf16[7,1152,512]{2,1,0:T(8,128)(2,1)S(1)} %get-tuple-element.11.wv, bf16[7,176,512]{2,1,0:T(8,128)(2,1)S(1)} %get-tuple-element.12.cv, bf16[576,1152]{1,0:T(8,128)(2,1)S(1)} %get-tuple-element.13.sel), custom_call_target="tpu_custom_call" | custom-call | flops 3000000000 | bytes 1000000 | tf_op jit(solution)/shard_map/pallas_call | solution.py:474
  71.4 1.2 %shard_map.70 = (bf16[81,2,3584]{2,1,0:T(2,128)(2,1)}, f32[9,3584]{1,0:T(8,128)}) custom-call(bf16[81,2,3584]{2,1,0:T(2,128)(2,1)S(1)} %get-tuple-element.14.projected, f32[9,3584]{1,0:T(8,128)S(1)} %get-tuple-element.15.weight_grad), custom_call_target="tpu_custom_call" | custom-call | tf_op jit(solution)/shard_map/pallas_call | solution.py:495

commit v6 on v4

--- a/solution.py
+++ b/solution.py
@@ -261,7 +261,7 @@
     everybody = here.greet([hop[a][d] for a in "xyz" for d in (1, 2, 3)] + [twin])
     pb[0:PADDED, :] = pooled[...]
 
-    grad_twin, pooled_twin = [], []
+    grad_twin = []
 
     def gelu_rows(values, cotangent):
         square = values * values
@@ -270,28 +270,23 @@
         slope = plus + (0.5 * values) * (1.0 - t * t) * (C0 + (3.0 * C0 * C1) * square)
         return (values * plus).astype(BF16), (cotangent * slope).astype(BF16)
 
+    def product(j):
+        pre[j % 2] = jnp.dot(pooled[...], wv[j], preferred_element_type=F32)
+
     def forward(j):
-        pre[...] = jnp.dot(pooled[...], wv[j], preferred_element_type=F32)
-
-        @pl.loop(0, 11)
-        def _(i):
-            rows = pl.ds(pl.multiple_of(i * 16, 16), 16)
-            act, grad = gelu_rows(pre[rows, :], cv[j, rows, :].astype(F32))
+        for i in range(11):
+            rows = slice(16 * i, 16 * i + 16)
+            act, grad = gelu_rows(pre[j % 2, rows, :], cv[j, rows, :].astype(F32))
             pa[j, rows, :] = act
             gr[j, rows, :] = grad
-
-        if j == 0:
-            everybody()
-            pooled_twin.append(send(pb.at[pl.ds(0, PADDED)], pb.at[pl.ds(PADDED, PADDED)], twin))
         grad_twin.append(send(gr.at[j, pl.ds(0, PADDED)], gr.at[j, pl.ds(PADDED, PADDED)], twin))
 
     def give(j):
-        @pl.loop(0, 10)
-        def _(i):
-            rows = pl.ds(pl.multiple_of(i * 16, 16), 16)
-            out_proj[pl.ds(i * 8, 8), :, pl.ds(j * CHUNK, CHUNK)] = pa[j, rows, :].reshape(8, 2, CHUNK)
-
-        out_proj[80, :, pl.ds(j * CHUNK, CHUNK)] = pa[j, 160:162, :]
+        for i in range(10):
+            out_proj[8 * i : 8 * i + 8, :, CHUNK * j : CHUNK * j + CHUNK] = (
+                pa[j, 16 * i : 16 * i + 16, :].reshape(8, 2, CHUNK)
+            )
+        out_proj[80, :, CHUNK * j : CHUNK * j + CHUNK] = pa[j, 160:162, :]
 
     msg = {}
 
@@ -375,20 +370,26 @@
                     total = total + r3[s, d, j].astype(F32)
                 out_grad[S3 * s : S3 * s + S3, j * CHUNK : j * CHUNK + CHUNK] = total
 
+    product(0)
+    everybody()
+    pooled_twin = send(pb.at[pl.ds(0, PADDED)], pb.at[pl.ds(PADDED, PADDED)], twin)
     forward(0)
-    pooled_twin[0].wait_recv()
+    product(1)
+    forward(1)
+    pooled_twin.wait_recv()
     pt[...] = lax.dot_general(
         sel[...], pb[...], (((1,), (1,)), ((), ())), preferred_element_type=F32
     ).astype(BF16)
+    product(2)
     backward(0)
-    forward(1)
     forward(2)
+    product(3)
     backward(1)
-    relay(0)
     forward(3)
     backward(2)
+    relay(0)
+    backward(3)
     relay(1)
-    backward(3)
     relay(2)
     finish(0)
     finish(1)
@@ -453,7 +454,7 @@
         in_specs=[vmem_spec] * 4,
         out_specs=(vmem_spec, vmem_spec),
         scratch_shapes=[
-            vm(4, PADDED, CHUNK), pltpu.VMEM((PADDED, CHUNK), F32),
+            vm(4, PADDED, CHUNK), pltpu.VMEM((2, PADDED, CHUNK), F32),
             vm(2 * PADDED, D), vm(576, 2 * PADDED), vm(4, 2 * PADDED, CHUNK),
             vm(3, 4, 8, S1, CHUNK),
             vm(3, 4, 2, S1, CHUNK), vm(3, 4, 2, S1, CHUNK), vm(3, 4, S1, CHUNK), vm(3, 4, S1, CHUNK),

time: 69.1 us -> 68.7 us (level)
  no operation moved by 1% of the time
where the time goes in v6:
time: 68.7 us; the launch traced here: 68.6 us
  Pallas kernels  67.8 us (99%)
  between operations  0.81 us (1%)
    pallas_call x1, Pallas kernels, per_device(): pl.pallas_call(main_kernel, out_shape=(pltpu.VMEM(cot.shape, BF16), pltpu...  39.9 us
    pallas_call x1, Pallas kernels, per_device(): pl.pallas_call(pool_kernel, out_shape=(vm(PADDED, D), vm(4, D, CHUNK), vm...  26.7 us

profile of v6, /device:TPU:0, one launch (start us, length us, event | category | flops | bytes accessed | tf_op | source)
XLA Modules:
  0.0 68.6 jit_solution(11992222714024005354)
XLA Ops:
  0.6 26.7 %shard_map.68 = (bf16[176,1152]{1,0:T(8,128)(2,1)S(1)}, bf16[4,1152,896]{2,1,0:T(8,128)(2,1)S(1)}, bf16[4,176,896]{2,1,0:T(8,128)(2,1)S(1)}, bf16[576,1152]{1,0:T(8,128)(2,1)S(1)}) custom-call(bf16[2,648,1152]{2,1,0:T(8,128)(2,1)} %bitcast.9, bf16[1152,3584]{1,0:T(8,128)(2,1)} %wgt.1, bf16[81,2,3584]{2,1,0:T(2,128)(2,1)} %bitcast.10, s32[2,256]{1,0:T(2,128)} %shots_in.1, ...), custom_call_target="tpu_custom_call" | custom-call | flops 1000000000 | bytes 14000000 | tf_op jit(solution)/shard_map/pallas_call | solution.py:434
  27.3 39.9 %shard_map.69 = (bf16[81,2,3584]{2,1,0:T(2,128)(2,1)S(1)}, f32[9,3584]{1,0:T(8,128)S(1)}) custom-call(bf16[176,1152]{1,0:T(8,128)(2,1)S(1)} %get-tuple-element.10.pooled, bf16[4,1152,896]{2,1,0:T(8,128)(2,1)S(1)} %get-tuple-element.11.wv, bf16[4,176,896]{2,1,0:T(8,128)(2,1)S(1)} %get-tuple-element.12.cv, bf16[576,1152]{1,0:T(8,128)(2,1)S(1)} %get-tuple-element.13.sel), custom_call_target="tpu_custom_call" | custom-call | flops 3000000000 | bytes 1000000 | tf_op jit(solution)/shard_map/pallas_call | solution.py:451
  67.3 1.2 %shard_map.70 = (bf16[81,2,3584]{2,1,0:T(2,128)(2,1)}, f32[9,3584]{1,0:T(8,128)}) custom-call(bf16[81,2,3584]{2,1,0:T(2,128)(2,1)S(1)} %get-tuple-element.14.projected, f32[9,3584]{1,0:T(8,128)S(1)} %get-tuple-element.15.weight_grad), custom_call_target="tpu_custom_call" | custom-call | tf_op jit(solution)/shard_map/pallas_call | solution.py:471

commit v7 on v6

--- a/solution.py
+++ b/solution.py
@@ -374,37 +374,34 @@
     everybody()
     pooled_twin = send(pb.at[pl.ds(0, PADDED)], pb.at[pl.ds(PADDED, PADDED)], twin)
     forward(0)
-    product(1)
-    forward(1)
+    for j in (1, 2, 3):
+        product(j)
+        forward(j)
     pooled_twin.wait_recv()
     pt[...] = lax.dot_general(
         sel[...], pb[...], (((1,), (1,)), ((), ())), preferred_element_type=F32
     ).astype(BF16)
-    product(2)
     backward(0)
-    forward(2)
-    product(3)
     backward(1)
-    forward(3)
     backward(2)
     relay(0)
     backward(3)
+    give(0)
     relay(1)
+    give(1)
     relay(2)
+    give(2)
+    relay(3)
+    give(3)
     finish(0)
     finish(1)
     second_stage(0)
-    relay(3)
-    give(0)
     finish(2)
     second_relay(0)
     finish(3)
     second_stage(1)
-    give(1)
     second_finish(0)
-    give(2)
     second_relay(1)
-    give(3)
     settle()
     second_finish(1)
     third_stage()

time: 68.7 us -> 68.6 us (level)
  no operation moved by 1% of the time
where the time goes in v7:
time: 68.6 us; the launch traced here: 68.5 us
  Pallas kernels  67.7 us (99%)
  between operations  0.81 us (1%)
    pallas_call x1, Pallas kernels, per_device(): pl.pallas_call(main_kernel, out_shape=(pltpu.VMEM(cot.shape, BF16), pltpu...  39.8 us
    pallas_call x1, Pallas kernels, per_device(): pl.pallas_call(pool_kernel, out_shape=(vm(PADDED, D), vm(4, D, CHUNK), vm...  26.7 us

profile of v7, /device:TPU:0, one launch (start us, length us, event | category | flops | bytes accessed | tf_op | source)
XLA Modules:
  0.0 68.5 jit_solution(8685032644585161104)
XLA Ops:
  0.6 26.7 %shard_map.68 = (bf16[176,1152]{1,0:T(8,128)(2,1)S(1)}, bf16[4,1152,896]{2,1,0:T(8,128)(2,1)S(1)}, bf16[4,176,896]{2,1,0:T(8,128)(2,1)S(1)}, bf16[576,1152]{1,0:T(8,128)(2,1)S(1)}) custom-call(bf16[2,648,1152]{2,1,0:T(8,128)(2,1)} %bitcast.9, bf16[1152,3584]{1,0:T(8,128)(2,1)} %wgt.1, bf16[81,2,3584]{2,1,0:T(2,128)(2,1)} %bitcast.10, s32[2,256]{1,0:T(2,128)} %shots_in.1, ...), custom_call_target="tpu_custom_call" | custom-call | flops 1000000000 | bytes 14000000 | tf_op jit(solution)/shard_map/pallas_call | solution.py:431
  27.3 39.8 %shard_map.69 = (bf16[81,2,3584]{2,1,0:T(2,128)(2,1)S(1)}, f32[9,3584]{1,0:T(8,128)S(1)}) custom-call(bf16[176,1152]{1,0:T(8,128)(2,1)S(1)} %get-tuple-element.10.pooled, bf16[4,1152,896]{2,1,0:T(8,128)(2,1)S(1)} %get-tuple-element.11.wv, bf16[4,176,896]{2,1,0:T(8,128)(2,1)S(1)} %get-tuple-element.12.cv, bf16[576,1152]{1,0:T(8,128)(2,1)S(1)} %get-tuple-element.13.sel), custom_call_target="tpu_custom_call" | custom-call | flops 3000000000 | bytes 1000000 | tf_op jit(solution)/shard_map/pallas_call | solution.py:448
  67.2 1.2 %shard_map.70 = (bf16[81,2,3584]{2,1,0:T(2,128)(2,1)}, f32[9,3584]{1,0:T(8,128)}) custom-call(bf16[81,2,3584]{2,1,0:T(2,128)(2,1)S(1)} %get-tuple-element.14.projected, f32[9,3584]{1,0:T(8,128)S(1)} %get-tuple-element.15.weight_grad), custom_call_target="tpu_custom_call" | custom-call | tf_op jit(solution)/shard_map/pallas_call | solution.py:468

commit v8 on v7

--- a/solution.py
+++ b/solution.py
@@ -25,7 +25,7 @@
 
 
 def add16(a, b):
-    return (a.astype(F32) + b.astype(F32)).astype(BF16)
+    return a + b
 
 
 class Place:
@@ -85,24 +85,26 @@
     return lax.broadcasted_iota(jnp.int32, shape, axis)
 
 
-def pool_kernel(
+def kernel(
     feat, wgt, cot, shots_in, band_in,
-    pb, wv, cv, sel,
-    fv, cn, kron, part,
+    out_proj, out_grad,
+    wv, cv, sel, fv, cn, kron, part,
     xa, xfu, xfd, xnu, xnd, yfu, yfd, ynu, ynd, sb, yx,
     ids_v, band_s,
+    pa, pre, pb, pt, gr, g,
+    ru, rd, nu, nd, r1, ru2, rd2, nu2, nd2, r2, r3,
     local_sem, send_sem, recv_sem,
 ):
     here = Place(local_sem, send_sem, recv_sem)
     core, x, y, z, lo = here.core, here.x, here.y, here.z, here.lo
-    hop, local, send = here.hop, here.local, here.send
+    hop, local, send, settle, twin = here.hop, here.local, here.send, here.settle, here.twin
     la, lb = pl.ds(0, XL), pl.ds(XL, YL)
     ids_in = local(shots_in, ids_v)
     width_in = local(band_in, band_s)
     feat_a = local(feat.at[:, :, la], fv.at[:, :, la])
     feat_b = local(feat.at[:, :, lb], fv.at[:, :, lb])
 
-    everybody = here.greet([hop["y"][1], hop["y"][3], here.mate])
+    everybody = here.greet([hop[a][d] for a in "xyz" for d in (1, 2, 3)] + [twin])
 
     frame, other = iota((BLOCK, 128), 0), iota((BLOCK, 128), 1)
     distance = jnp.abs(frame - other)
@@ -244,22 +246,7 @@
         part[0, 0, :, XL:D].astype(F32) + ynu[0].astype(F32) + ynd[0].astype(F32) + yx[...].astype(F32),
         slice(XL, D),
     )
-    for copy in wgt_in:
-        copy.wait()
-    here.settle()
-
-
-def main_kernel(
-    pooled, wv, cv, sel,
-    out_proj, out_grad,
-    pa, pre, pb, pt, gr, g,
-    ru, rd, nu, nd, r1, ru2, rd2, nu2, nd2, r2, r3,
-    send_sem, recv_sem,
-):
-    here = Place(None, send_sem, recv_sem)
-    hop, send, settle, twin = here.hop, here.send, here.settle, here.twin
-    everybody = here.greet([hop[a][d] for a in "xyz" for d in (1, 2, 3)] + [twin])
-    pb[0:PADDED, :] = pooled[...]
+    pooled_twin = send(pb.at[pl.ds(0, PADDED)], pb.at[pl.ds(PADDED, PADDED)], twin)
 
     grad_twin = []
 
@@ -271,7 +258,7 @@
         return (values * plus).astype(BF16), (cotangent * slope).astype(BF16)
 
     def product(j):
-        pre[j % 2] = jnp.dot(pooled[...], wv[j], preferred_element_type=F32)
+        pre[j % 2] = jnp.dot(pb[0:PADDED, :], wv[j], preferred_element_type=F32)
 
     def forward(j):
         for i in range(11):
@@ -279,6 +266,8 @@
             act, grad = gelu_rows(pre[j % 2, rows, :], cv[j, rows, :].astype(F32))
             pa[j, rows, :] = act
             gr[j, rows, :] = grad
+
+    def share(j):
         grad_twin.append(send(gr.at[j, pl.ds(0, PADDED)], gr.at[j, pl.ds(PADDED, PADDED)], twin))
 
     def give(j):
@@ -370,13 +359,16 @@
                     total = total + r3[s, d, j].astype(F32)
                 out_grad[S3 * s : S3 * s + S3, j * CHUNK : j * CHUNK + CHUNK] = total
 
+    settle()
+    for copy in wgt_in:
+        copy.wait()
     product(0)
-    everybody()
-    pooled_twin = send(pb.at[pl.ds(0, PADDED)], pb.at[pl.ds(PADDED, PADDED)], twin)
-    forward(0)
-    for j in (1, 2, 3):
-        product(j)
+    for j in range(3):
+        product(j + 1)
         forward(j)
+        share(j)
+    forward(3)
+    share(3)
     pooled_twin.wait_recv()
     pt[...] = lax.dot_general(
         sel[...], pb[...], (((1,), (1,)), ((), ())), preferred_element_type=F32
@@ -386,25 +378,25 @@
     backward(2)
     relay(0)
     backward(3)
-    give(0)
     relay(1)
-    give(1)
     relay(2)
-    give(2)
+    finish(0)
     relay(3)
-    give(3)
-    finish(0)
     finish(1)
     second_stage(0)
     finish(2)
     second_relay(0)
     finish(3)
     second_stage(1)
+    give(0)
+    give(1)
     second_finish(0)
     second_relay(1)
+    give(2)
     settle()
     second_finish(1)
     third_stage()
+    give(3)
     owned()
     settle()
 
@@ -428,29 +420,17 @@
     any_spec = pl.BlockSpec(memory_space=pl.ANY)
     vmem_spec = pl.BlockSpec(memory_space=pltpu.VMEM)
     pin = lambda space, *arrays: [pltpu.with_memory_space_constraint(a, space) for a in arrays]
-    shared = pl.pallas_call(
-        pool_kernel,
-        out_shape=(vm(PADDED, D), vm(4, D, CHUNK), vm(4, PADDED, CHUNK), vm(576, D)),
+    projected, weight_grad = pl.pallas_call(
+        kernel,
+        out_shape=(pltpu.VMEM(cot.shape, BF16), pltpu.VMEM((9, H), F32)),
         in_specs=[any_spec] * 5,
-        out_specs=(vmem_spec,) * 4,
+        out_specs=(vmem_spec, vmem_spec),
         scratch_shapes=[
+            vm(4, D, CHUNK), vm(4, PADDED, CHUNK), vm(576, D),
             vm(2, TOKS * POOL, D), vm(4, TOKS, 2, CHUNK), vm(256, 256), vm(4, 2, ROWS, D),
             vm(4, ROWS, XL), vm(ROWS, XL // 2), vm(ROWS, XL // 2), vm(ROWS, XL), vm(ROWS, XL),
             vm(ROWS, YL), vm(ROWS, YL), vm(2, ROWS, YL), vm(2, ROWS, YL), vm(ROWS, YL), vm(ROWS, YL),
             pltpu.VMEM(shot_ids.shape, jnp.int32), pltpu.SMEM(band_width.shape, jnp.int32),
-            sems(12), sems(24), sems(24),
-        ],
-        compiler_params=pltpu.CompilerParams(
-            collective_id=0, has_side_effects=True, vmem_limit_bytes=24 * 1024 * 1024
-        ),
-        cost_estimate=pl.CostEstimate(flops=10**9, bytes_accessed=14 * 10**6, transcendentals=0),
-    )(*pin(pltpu.HBM, frames, proj_weight, cot, shot_ids, band_width))
-    projected, weight_grad = pl.pallas_call(
-        main_kernel,
-        out_shape=(pltpu.VMEM(cot.shape, BF16), pltpu.VMEM((9, H), F32)),
-        in_specs=[vmem_spec] * 4,
-        out_specs=(vmem_spec, vmem_spec),
-        scratch_shapes=[
             vm(4, PADDED, CHUNK), pltpu.VMEM((2, PADDED, CHUNK), F32),
             vm(2 * PADDED, D), vm(576, 2 * PADDED), vm(4, 2 * PADDED, CHUNK),
             vm(3, 4, 8, S1, CHUNK),
@@ -458,13 +438,15 @@
             vm(3, 2, 8, S2, CHUNK), vm(3, 2, 2, S2, CHUNK), vm(3, 2, 2, S2, CHUNK),
             vm(3, 2, S2, CHUNK), vm(3, 2, S2, CHUNK),
             vm(3, 4, 4, S3, CHUNK), vm(3, 4, 4, S3, CHUNK),
-            sems(88), sems(88),
+            sems(12), sems(108), sems(108),
         ],
         compiler_params=pltpu.CompilerParams(
-            collective_id=1, has_side_effects=True, vmem_limit_bytes=36 * 1024 * 1024
+            collective_id=0, has_side_effects=True, vmem_limit_bytes=50 * 1024 * 1024
         ),
-        cost_estimate=pl.CostEstimate(flops=3 * 10**9, bytes_accessed=10**6, transcendentals=600000),
-    )(*pin(pltpu.VMEM, *shared))
+        cost_estimate=pl.CostEstimate(
+            flops=4 * 10**9, bytes_accessed=14 * 10**6, transcendentals=600000
+        ),
+    )(*pin(pltpu.HBM, frames, proj_weight, cot, shot_ids, band_width))
     projected, weight_grad = pl.pallas_call(
         hand_over,
         out_shape=(

time: 68.6 us -> 68.4 us (level)
    pallas_call x2 -> x1, Pallas kernels: 66.5 us -> 66.3 us  [per_device(): pl.pallas_call(kernel, out_shape=(pltpu.VMEM(cot.shape, BF16), pltpu.VMEM...]
where the time goes in v8:
time: 68.4 us; the launch traced here: 68.2 us
  Pallas kernels  67.4 us (99%)
  between operations  0.8 us (1%)
    pallas_call x1, Pallas kernels, per_device(): pl.pallas_call(kernel, out_shape=(pltpu.VMEM(cot.shape, BF16), pltpu.VMEM...  66.3 us

profile of v8, /device:TPU:0, one launch (start us, length us, event | category | flops | bytes accessed | tf_op | source)
XLA Modules:
  0.0 68.2 jit_solution(18187645219833932214)
XLA Ops:
  0.6 66.3 %shard_map.68 = (bf16[81,2,3584]{2,1,0:T(2,128)(2,1)S(1)}, f32[9,3584]{1,0:T(8,128)S(1)}) custom-call(bf16[2,648,1152]{2,1,0:T(8,128)(2,1)} %bitcast.9, bf16[1152,3584]{1,0:T(8,128)(2,1)} %wgt.1, bf16[81,2,3584]{2,1,0:T(2,128)(2,1)} %bitcast.10, s32[2,256]{1,0:T(2,128)} %shots_in.1, s32[2,4]{1,0:T(2,128)} %band_in.1), custom_call_target="tpu_custom_call" | custom-call | flops 4000000000 | bytes 14000000 | tf_op jit(solution)/shard_map/pallas_call | solution.py:423
  66.9 1.2 %shard_map.69 = (bf16[81,2,3584]{2,1,0:T(2,128)(2,1)}, f32[9,3584]{1,0:T(8,128)}) custom-call(bf16[81,2,3584]{2,1,0:T(2,128)(2,1)S(1)} %get-tuple-element.6.projected, f32[9,3584]{1,0:T(8,128)S(1)} %get-tuple-element.7.weight_grad), custom_call_target="tpu_custom_call" | custom-call | tf_op jit(solution)/shard_map/pallas_call | solution.py:450

commit v9 on v8

--- a/solution.py
+++ b/solution.py
@@ -92,7 +92,7 @@
     xa, xfu, xfd, xnu, xnd, yfu, yfd, ynu, ynd, sb, yx,
     ids_v, band_s,
     pa, pre, pb, pt, gr, g,
-    ru, rd, nu, nd, r1, ru2, rd2, nu2, nd2, r2, r3,
+    ru, rd, nu, nd, r1, in2, r2, r3,
     local_sem, send_sem, recv_sem,
 ):
     here = Place(local_sem, send_sem, recv_sem)
@@ -309,40 +309,27 @@
             msg["nd", s, j] = send(rd.at[s, j, 0], nd.at[s, j], to[3])
 
     def finish(j):
-        q, k = j // 2, j % 2
         for s in range(3):
             wait(("nu", s, j), ("nd", s, j))
             for h, value in enumerate(
                 (add3(g[s, j, 6], nu[s, j], rd[s, j, 1]), add3(g[s, j, 7], ru[s, j, 1], nd[s, j]))
             ):
                 for b in range(2):
-                    slot = SLOTS.index((2 * h + b, k))
-                    r1[s, q, slot] = value[S2 * b : S2 * b + S2].astype(BF16)
+                    r1[s, 2 * h + b, j] = value[S2 * b : S2 * b + S2].astype(BF16)
 
     def second_stage(q):
-        for s in range(3):
-            to = hop[ORDER[s][1]]
-            msg["ru2", s, q] = send(r1.at[s, q, pl.ds(0, 2)], ru2.at[s, q], to[1])
-            msg["rd2", s, q] = send(r1.at[s, q, pl.ds(2, 2)], rd2.at[s, q], to[3])
-
-    def second_relay(q):
-        for s in range(3):
-            to = hop[ORDER[s][1]]
-            wait(("ru2", s, q))
-            ru2[s, q, 0] = add16(ru2[s, q, 0], r1[s, q, 4])
-            msg["nu2", s, q] = send(ru2.at[s, q, 0], nu2.at[s, q], to[1])
-            wait(("rd2", s, q))
-            rd2[s, q, 0] = add16(rd2[s, q, 0], r1[s, q, 5])
-            msg["nd2", s, q] = send(rd2.at[s, q, 0], nd2.at[s, q], to[3])
+        steps = pl.ds(2 * q, 2)
+        for d in (2, 1, 3):
+            for s in range(3):
+                msg["second", s, q, d] = send(r1.at[s, d, steps], in2.at[s, d, steps], hop[ORDER[s][1]][d])
 
     def second_finish(q):
         for s in range(3):
-            wait(("nu2", s, q), ("nd2", s, q))
-            for k, value in enumerate(
-                (add3(r1[s, q, 6], nu2[s, q], rd2[s, q, 1]), add3(r1[s, q, 7], ru2[s, q, 1], nd2[s, q]))
-            ):
+            wait(*(("second", s, q, d) for d in (1, 2, 3)))
+            for j in (2 * q, 2 * q + 1):
+                value = add3(r1[s, 0, j], in2[s, 1, j], in2[s, 3, j]) + in2[s, 2, j].astype(F32)
                 for c in range(4):
-                    r2[s, c, 2 * q + k] = value[S3 * c : S3 * c + S3].astype(BF16)
+                    r2[s, c, j] = value[S3 * c : S3 * c + S3].astype(BF16)
 
     def third_stage():
         for s in range(3):
@@ -362,37 +349,38 @@
     settle()
     for copy in wgt_in:
         copy.wait()
-    product(0)
-    for j in range(3):
-        product(j + 1)
+
+    def step(j):
+        product(j)
         forward(j)
         share(j)
-    forward(3)
-    share(3)
+
+    step(0)
+    step(1)
     pooled_twin.wait_recv()
     pt[...] = lax.dot_general(
         sel[...], pb[...], (((1,), (1,)), ((), ())), preferred_element_type=F32
     ).astype(BF16)
     backward(0)
+    step(2)
     backward(1)
+    step(3)
+    relay(0)
     backward(2)
-    relay(0)
+    relay(1)
     backward(3)
-    relay(1)
+    give(0)
     relay(2)
+    give(1)
     finish(0)
-    relay(3)
     finish(1)
     second_stage(0)
+    relay(3)
+    give(2)
     finish(2)
-    second_relay(0)
     finish(3)
     second_stage(1)
-    give(0)
-    give(1)
     second_finish(0)
-    second_relay(1)
-    give(2)
     settle()
     second_finish(1)
     third_stage()
@@ -435,8 +423,7 @@
             vm(2 * PADDED, D), vm(576, 2 * PADDED), vm(4, 2 * PADDED, CHUNK),
             vm(3, 4, 8, S1, CHUNK),
             vm(3, 4, 2, S1, CHUNK), vm(3, 4, 2, S1, CHUNK), vm(3, 4, S1, CHUNK), vm(3, 4, S1, CHUNK),
-            vm(3, 2, 8, S2, CHUNK), vm(3, 2, 2, S2, CHUNK), vm(3, 2, 2, S2, CHUNK),
-            vm(3, 2, S2, CHUNK), vm(3, 2, S2, CHUNK),
+            vm(3, 4, 4, S2, CHUNK), vm(3, 4, 4, S2, CHUNK),
             vm(3, 4, 4, S3, CHUNK), vm(3, 4, 4, S3, CHUNK),
             sems(12), sems(108), sems(108),
         ],

time: 68.4 us -> 65.5 us (0.958)
  Pallas kernels: 67.4 us -> 64.6 us
    pallas_call x1, Pallas kernels: 66.3 us -> 63.4 us  [per_device(): pl.pallas_call(kernel, out_shape=(pltpu.VMEM(cot.shape, BF16), pltpu.VMEM...]
where the time goes in v9:
time: 65.5 us; the launch traced here: 65.4 us
  Pallas kernels  64.6 us (99%)
  between operations  0.8 us (1%)
    pallas_call x1, Pallas kernels, per_device(): pl.pallas_call(kernel, out_shape=(pltpu.VMEM(cot.shape, BF16), pltpu.VMEM...  63.4 us

profile of v9, /device:TPU:0, one launch (start us, length us, event | category | flops | bytes accessed | tf_op | source)
XLA Modules:
  0.0 65.4 jit_solution(12571733598924385966)
XLA Ops:
  0.6 63.4 %shard_map.68 = (bf16[81,2,3584]{2,1,0:T(2,128)(2,1)S(1)}, f32[9,3584]{1,0:T(8,128)S(1)}) custom-call(bf16[2,648,1152]{2,1,0:T(8,128)(2,1)} %bitcast.9, bf16[1152,3584]{1,0:T(8,128)(2,1)} %wgt.1, bf16[81,2,3584]{2,1,0:T(2,128)(2,1)} %bitcast.10, s32[2,256]{1,0:T(2,128)} %shots_in.1, s32[2,4]{1,0:T(2,128)} %band_in.1), custom_call_target="tpu_custom_call" | custom-call | flops 4000000000 | bytes 14000000 | tf_op jit(solution)/shard_map/pallas_call | solution.py:411
  64.1 1.2 %shard_map.69 = (bf16[81,2,3584]{2,1,0:T(2,128)(2,1)}, f32[9,3584]{1,0:T(8,128)}) custom-call(bf16[81,2,3584]{2,1,0:T(2,128)(2,1)S(1)} %get-tuple-element.6.projected, f32[9,3584]{1,0:T(8,128)S(1)} %get-tuple-element.7.weight_grad), custom_call_target="tpu_custom_call" | custom-call | tf_op jit(solution)/shard_map/pallas_call | solution.py:437

commit v10 on v9

--- a/solution.py
+++ b/solution.py
@@ -16,7 +16,9 @@
 PADDED = 176
 XL = 512
 YL = D - XL
-CHUNK = H // 4
+STEPS = ((0, 1024), (1024, 1024), (2048, 1024), (3072, 512))
+WIDEST = 1024
+GROUPS = ((0, 3072), (3072, 512))
 ORDER = (("z", "y", "x"), ("y", "x", "z"), ("x", "z", "y"))
 SLOTS = ((2, 0), (1, 1), (2, 1), (3, 0), (1, 0), (3, 1), (0, 0), (0, 1))
 S1, S2, S3 = 24, 12, 3
@@ -153,19 +155,23 @@
     up, down, side = hop["y"][1], hop["y"][3], here.mate
 
     feat_a.wait()
-    partial_sums(slice(0, XL))
+    partial_sums(slice(0, XL // 2))
     everybody()
-    x_first = {dy: send(part.at[dy, 1, :, la], xa.at[dy], side) for dy in (2, 1, 3, 0)}
+    x_first = {dy: [send(part.at[dy, 1, :, l1], xa.at[dy, :, l1], side)] for dy in (2, 1, 3, 0)}
     feat_b.wait()
     partial_sums(slice(XL, D))
     far_up = send(part.at[2, 0, :, lb], yfu, up)
     far_down = send(part.at[2, 1, :, lb], yfd, down)
     near_up = {1: send(part.at[1, 1, :, lb], ynu.at[1], up)}
     near_down = {0: send(part.at[3, 0, :, lb], ynd.at[0], down)}
-
-    columns = [pl.ds(j * CHUNK, CHUNK) for j in range(4)]
-    cot_in = [local(cot.at[:, :, columns[j]], cn.at[j]) for j in range(4)]
-    wgt_in = [local(wgt.at[:, columns[j]], wv.at[j]) for j in range(4)]
+    partial_sums(slice(XL // 2, XL))
+    for dy in (2, 1, 3, 0):
+        x_first[dy].append(send(part.at[dy, 1, :, l2], xa.at[dy, :, l2], side))
+
+    cols = [slice(c, c + w) for c, w in STEPS]
+    window = [pl.ds(c, w) for c, w in STEPS]
+    cot_in = local(cot, cn)
+    wgt_in = [local(wgt.at[:, c], wv.at[:, c]) for c in window]
 
     row, lane = iota((576, 128), 0), iota((576, 128), 1)
     which, slot = lax.div(row, 192), lax.div(lax.rem(row, 192), S1)
@@ -187,7 +193,8 @@
         sel[:, 128 * k : 128 * k + 128] = jnp.where(wanted == lane + 128 * k, 1.0, 0.0).astype(BF16)
 
     def take(dy):
-        x_first[dy].wait_recv()
+        for copy in x_first[dy]:
+            copy.wait_recv()
         xa[dy] = add16(xa[dy], part[dy, 0, :, 0:XL])
 
     take(2)
@@ -204,15 +211,14 @@
     take(3)
     near_down2 = [send(xa.at[3, :, l1], xnd.at[:, l1], down)]
 
-    for j in range(4):
-        cot_in[j].wait()
-
-        @pl.loop(0, 10)
-        def _(i):
-            cv[j, pl.ds(pl.multiple_of(i * 16, 16), 16), :] = cn[j, pl.ds(i * 8, 8)].reshape(16, CHUNK)
-
-        tail = jnp.concatenate([cn[j, 80].astype(F32), jnp.zeros((14, CHUNK), F32)], axis=0)
-        cv[j, 160:176, :] = tail.astype(BF16)
+    cot_in.wait()
+
+    @pl.loop(0, 10)
+    def _(i):
+        cv[pl.ds(pl.multiple_of(i * 16, 16), 16), :] = cn[pl.ds(i * 8, 8)].reshape(16, H)
+
+    cot_tail = jnp.concatenate([cn[80].astype(F32), jnp.zeros((14, H), F32)], axis=0)
+    cv[160:176, :] = cot_tail.astype(BF16)
 
     far_up2.wait_recv()
     xfu[...] = add16(xfu[...], xa[1, :, 0 : XL // 2])
@@ -258,24 +264,25 @@
         return (values * plus).astype(BF16), (cotangent * slope).astype(BF16)
 
     def product(j):
-        pre[j % 2] = jnp.dot(pb[0:PADDED, :], wv[j], preferred_element_type=F32)
+        pre[j % 2, :, 0 : STEPS[j][1]] = jnp.dot(pb[0:PADDED, :], wv[:, cols[j]], preferred_element_type=F32)
 
     def forward(j):
         for i in range(11):
             rows = slice(16 * i, 16 * i + 16)
-            act, grad = gelu_rows(pre[j % 2, rows, :], cv[j, rows, :].astype(F32))
-            pa[j, rows, :] = act
-            gr[j, rows, :] = grad
+            act, grad = gelu_rows(pre[j % 2, rows, 0 : STEPS[j][1]], cv[rows, cols[j]].astype(F32))
+            pa[rows, cols[j]] = act
+            gr[rows, cols[j]] = grad
 
     def share(j):
-        grad_twin.append(send(gr.at[j, pl.ds(0, PADDED)], gr.at[j, pl.ds(PADDED, PADDED)], twin))
+        grad_twin.append(
+            send(gr.at[pl.ds(0, PADDED), window[j]], gr.at[pl.ds(PADDED, PADDED), window[j]], twin)
+        )
 
     def give(j):
         for i in range(10):
-            out_proj[8 * i : 8 * i + 8, :, CHUNK * j : CHUNK * j + CHUNK] = (
-                pa[j, 16 * i : 16 * i + 16, :].reshape(8, 2, CHUNK)
-            )
-        out_proj[80, :, CHUNK * j : CHUNK * j + CHUNK] = pa[j, 160:162, :]
+            rows = pa[16 * i : 16 * i + 16, cols[j]]
+            out_proj[8 * i : 8 * i + 8, :, cols[j]] = rows.reshape(8, 2, STEPS[j][1])
+        out_proj[80, :, cols[j]] = pa[160:162, cols[j]]
 
     msg = {}
 
@@ -288,63 +295,67 @@
 
     def backward(j):
         grad_twin[j].wait_recv()
-        got = jnp.dot(pt[...], gr[j], preferred_element_type=F32)
+        got = jnp.dot(pt[...], gr[:, cols[j]], preferred_element_type=F32)
         for s in range(3):
             for p in range(8):
                 base = s * 192 + p * S1
-                g[s, j, p] = got[base : base + S1].astype(BF16)
+                g[s, p, :, cols[j]] = got[base : base + S1].astype(BF16)
+        c = window[j]
         for s in range(3):
             to = hop[ORDER[s][0]]
-            msg["ru", s, j] = send(g.at[s, j, pl.ds(0, 2)], ru.at[s, j], to[1])
-            msg["rd", s, j] = send(g.at[s, j, pl.ds(2, 2)], rd.at[s, j], to[3])
+            msg["ru", s, j] = send(g.at[s, pl.ds(0, 2), :, c], ru.at[s, :, :, c], to[1])
+            msg["rd", s, j] = send(g.at[s, pl.ds(2, 2), :, c], rd.at[s, :, :, c], to[3])
 
     def relay(j):
+        c, w = cols[j], window[j]
         for s in range(3):
             to = hop[ORDER[s][0]]
             wait(("ru", s, j))
-            ru[s, j, 0] = add16(ru[s, j, 0], g[s, j, 4])
-            msg["nu", s, j] = send(ru.at[s, j, 0], nu.at[s, j], to[1])
+            ru[s, 0, :, c] = add16(ru[s, 0, :, c], g[s, 4, :, c])
+            msg["nu", s, j] = send(ru.at[s, 0, :, w], nu.at[s, :, w], to[1])
             wait(("rd", s, j))
-            rd[s, j, 0] = add16(rd[s, j, 0], g[s, j, 5])
-            msg["nd", s, j] = send(rd.at[s, j, 0], nd.at[s, j], to[3])
+            rd[s, 0, :, c] = add16(rd[s, 0, :, c], g[s, 5, :, c])
+            msg["nd", s, j] = send(rd.at[s, 0, :, w], nd.at[s, :, w], to[3])
 
     def finish(j):
+        c = cols[j]
         for s in range(3):
             wait(("nu", s, j), ("nd", s, j))
             for h, value in enumerate(
-                (add3(g[s, j, 6], nu[s, j], rd[s, j, 1]), add3(g[s, j, 7], ru[s, j, 1], nd[s, j]))
+                (
+                    add3(g[s, 6, :, c], nu[s, :, c], rd[s, 1, :, c]),
+                    add3(g[s, 7, :, c], ru[s, 1, :, c], nd[s, :, c]),
+                )
             ):
                 for b in range(2):
-                    r1[s, 2 * h + b, j] = value[S2 * b : S2 * b + S2].astype(BF16)
+                    r1[s, 2 * h + b, :, c] = value[S2 * b : S2 * b + S2].astype(BF16)
 
     def second_stage(q):
-        steps = pl.ds(2 * q, 2)
+        c = pl.ds(*GROUPS[q])
         for d in (2, 1, 3):
             for s in range(3):
-                msg["second", s, q, d] = send(r1.at[s, d, steps], in2.at[s, d, steps], hop[ORDER[s][1]][d])
-
-    def second_finish(q):
+                to = hop[ORDER[s][1]][d]
+                msg["second", s, q, d] = send(r1.at[s, d, :, c], in2.at[s, d, :, c], to)
+
+    def third_stage(q):
+        c = slice(GROUPS[q][0], sum(GROUPS[q]))
         for s in range(3):
             wait(*(("second", s, q, d) for d in (1, 2, 3)))
-            for j in (2 * q, 2 * q + 1):
-                value = add3(r1[s, 0, j], in2[s, 1, j], in2[s, 3, j]) + in2[s, 2, j].astype(F32)
-                for c in range(4):
-                    r2[s, c, j] = value[S3 * c : S3 * c + S3].astype(BF16)
-
-    def third_stage():
-        for s in range(3):
-            to = hop[ORDER[s][2]]
+            value = add3(r1[s, 0, :, c], in2[s, 1, :, c], in2[s, 3, :, c]) + in2[s, 2, :, c].astype(F32)
+            for d in range(4):
+                r2[s, d, :, c] = value[S3 * d : S3 * d + S3].astype(BF16)
+            w = pl.ds(*GROUPS[q])
             for d in (2, 1, 3):
-                msg["last", s, d] = send(r2.at[s, d], r3.at[s, d], to[d])
-
-    def owned():
-        for s in range(3):
-            wait(*(("last", s, d) for d in (1, 2, 3)))
-            for j in range(4):
-                total = r2[s, 0, j].astype(F32)
-                for d in (1, 2, 3):
-                    total = total + r3[s, d, j].astype(F32)
-                out_grad[S3 * s : S3 * s + S3, j * CHUNK : j * CHUNK + CHUNK] = total
+                msg["last", s, q, d] = send(r2.at[s, d, :, w], r3.at[s, d, :, w], hop[ORDER[s][2]][d])
+
+    def owned(q):
+        c = slice(GROUPS[q][0], sum(GROUPS[q]))
+        for s in range(3):
+            wait(*(("last", s, q, d) for d in (1, 2, 3)))
+            total = r2[s, 0, :, c].astype(F32)
+            for d in (1, 2, 3):
+                total = total + r3[s, d, :, c].astype(F32)
+            out_grad[S3 * s : S3 * s + S3, c] = total
 
     settle()
     for copy in wgt_in:
@@ -369,23 +380,23 @@
     backward(2)
     relay(1)
     backward(3)
+    relay(2)
+    finish(0)
+    relay(3)
+    finish(1)
+    finish(2)
+    second_stage(0)
     give(0)
-    relay(2)
-    give(1)
-    finish(0)
-    finish(1)
-    second_stage(0)
-    relay(3)
-    give(2)
-    finish(2)
     finish(3)
     second_stage(1)
-    second_finish(0)
+    give(1)
+    third_stage(0)
+    give(2)
     settle()
-    second_finish(1)
-    third_stage()
+    third_stage(1)
     give(3)
-    owned()
+    owned(0)
+    owned(1)
     settle()
 
 
@@ -414,18 +425,16 @@
         in_specs=[any_spec] * 5,
         out_specs=(vmem_spec, vmem_spec),
         scratch_shapes=[
-            vm(4, D, CHUNK), vm(4, PADDED, CHUNK), vm(576, D),
-            vm(2, TOKS * POOL, D), vm(4, TOKS, 2, CHUNK), vm(256, 256), vm(4, 2, ROWS, D),
+            vm(D, H), vm(PADDED, H), vm(576, D),
+            vm(2, TOKS * POOL, D), vm(TOKS, 2, H), vm(256, 256), vm(4, 2, ROWS, D),
             vm(4, ROWS, XL), vm(ROWS, XL // 2), vm(ROWS, XL // 2), vm(ROWS, XL), vm(ROWS, XL),
             vm(ROWS, YL), vm(ROWS, YL), vm(2, ROWS, YL), vm(2, ROWS, YL), vm(ROWS, YL), vm(ROWS, YL),
             pltpu.VMEM(shot_ids.shape, jnp.int32), pltpu.SMEM(band_width.shape, jnp.int32),
-            vm(4, PADDED, CHUNK), pltpu.VMEM((2, PADDED, CHUNK), F32),
-            vm(2 * PADDED, D), vm(576, 2 * PADDED), vm(4, 2 * PADDED, CHUNK),
-            vm(3, 4, 8, S1, CHUNK),
-            vm(3, 4, 2, S1, CHUNK), vm(3, 4, 2, S1, CHUNK), vm(3, 4, S1, CHUNK), vm(3, 4, S1, CHUNK),
-            vm(3, 4, 4, S2, CHUNK), vm(3, 4, 4, S2, CHUNK),
-            vm(3, 4, 4, S3, CHUNK), vm(3, 4, 4, S3, CHUNK),
-            sems(12), sems(108), sems(108),
+            vm(PADDED, H), pltpu.VMEM((2, PADDED, WIDEST), F32),
+            vm(2 * PADDED, D), vm(576, 2 * PADDED), vm(2 * PADDED, H),
+            vm(3, 8, S1, H), vm(3, 2, S1, H), vm(3, 2, S1, H), vm(3, S1, H), vm(3, S1, H),
+            vm(3, 4, S2, H), vm(3, 4, S2, H), vm(3, 4, S3, H), vm(3, 4, S3, H),
+            sems(12), sems(128), sems(128),
         ],
         compiler_params=pltpu.CompilerParams(
             collective_id=0, has_side_effects=True, vmem_limit_bytes=50 * 1024 * 1024

time: 65.5 us -> 67.6 us (1.032)
  Pallas kernels: 64.6 us -> 66.7 us
    pallas_call x1, Pallas kernels: 63.4 us -> 65.5 us  [per_device(): pl.pallas_call(kernel, out_shape=(pltpu.VMEM(cot.shape, BF16), pltpu.VMEM...]
where the time goes in v10:
time: 67.6 us; the launch traced here: 67.5 us
  Pallas kernels  66.7 us (99%)
  between operations  0.8 us (1%)
    pallas_call x1, Pallas kernels, per_device(): pl.pallas_call(kernel, out_shape=(pltpu.VMEM(cot.shape, BF16), pltpu.VMEM...  65.5 us

profile of v10, /device:TPU:0, one launch (start us, length us, event | category | flops | bytes accessed | tf_op | source)
XLA Modules:
  0.0 67.5 jit_solution(9909157638932785365)
XLA Ops:
  0.6 65.5 %shard_map.68 = (bf16[81,2,3584]{2,1,0:T(2,128)(2,1)S(1)}, f32[9,3584]{1,0:T(8,128)S(1)}) custom-call(bf16[2,648,1152]{2,1,0:T(8,128)(2,1)} %bitcast.9, bf16[1152,3584]{1,0:T(8,128)(2,1)} %wgt.1, bf16[81,2,3584]{2,1,0:T(2,128)(2,1)} %bitcast.10, s32[2,256]{1,0:T(2,128)} %shots_in.1, s32[2,4]{1,0:T(2,128)} %band_in.1), custom_call_target="tpu_custom_call" | custom-call | flops 4000000000 | bytes 14000000 | tf_op jit(solution)/shard_map/pallas_call | solution.py:422
  66.2 1.2 %shard_map.69 = (bf16[81,2,3584]{2,1,0:T(2,128)(2,1)}, f32[9,3584]{1,0:T(8,128)}) custom-call(bf16[81,2,3584]{2,1,0:T(2,128)(2,1)S(1)} %get-tuple-element.6.projected, f32[9,3584]{1,0:T(8,128)S(1)} %get-tuple-element.7.weight_grad), custom_call_target="tpu_custom_call" | custom-call | tf_op jit(solution)/shard_map/pallas_call | solution.py:446

commit v11 on v10

--- a/solution.py
+++ b/solution.py
@@ -16,12 +16,14 @@
 PADDED = 176
 XL = 512
 YL = D - XL
-STEPS = ((0, 1024), (1024, 1024), (2048, 1024), (3072, 512))
-WIDEST = 1024
-GROUPS = ((0, 3072), (3072, 512))
+MINE = H // 2
+STEPS = ((0, 512), (512, 512), (1024, 512), (1536, 256))
+WIDEST = 512
+GROUPS = ((0, 1536), (1536, 256))
+DEPTH = 256
 ORDER = (("z", "y", "x"), ("y", "x", "z"), ("x", "z", "y"))
 SLOTS = ((2, 0), (1, 1), (2, 1), (3, 0), (1, 0), (3, 1), (0, 0), (0, 1))
-S1, S2, S3 = 24, 12, 3
+S1, S2, S3 = 48, 24, 6
 C0 = 0.7978845608028654
 C1 = 0.044715
 
@@ -90,11 +92,11 @@
 def kernel(
     feat, wgt, cot, shots_in, band_in,
     out_proj, out_grad,
-    wv, cv, sel, fv, cn, kron, part,
+    wv, cv, cx, sel, fv, cn, kron, part,
     xa, xfu, xfd, xnu, xnd, yfu, yfd, ynu, ynd, sb, yx,
     ids_v, band_s,
-    pa, pre, pb, pt, gr, g,
-    ru, rd, nu, nd, r1, in2, r2, r3,
+    pa, px, pre, pb, pt, gr, g,
+    ru, rd, nu, nd, r1, in2, r2, r3, own, fin, fin_twin,
     local_sem, send_sem, recv_sem,
 ):
     here = Place(local_sem, send_sem, recv_sem)
@@ -155,26 +157,24 @@
     up, down, side = hop["y"][1], hop["y"][3], here.mate
 
     feat_a.wait()
-    partial_sums(slice(0, XL // 2))
+    partial_sums(slice(0, XL))
     everybody()
-    x_first = {dy: [send(part.at[dy, 1, :, l1], xa.at[dy, :, l1], side)] for dy in (2, 1, 3, 0)}
+    x_first = {dy: send(part.at[dy, 1, :, la], xa.at[dy], side) for dy in (2, 1, 3, 0)}
     feat_b.wait()
     partial_sums(slice(XL, D))
     far_up = send(part.at[2, 0, :, lb], yfu, up)
     far_down = send(part.at[2, 1, :, lb], yfd, down)
     near_up = {1: send(part.at[1, 1, :, lb], ynu.at[1], up)}
     near_down = {0: send(part.at[3, 0, :, lb], ynd.at[0], down)}
-    partial_sums(slice(XL // 2, XL))
-    for dy in (2, 1, 3, 0):
-        x_first[dy].append(send(part.at[dy, 1, :, l2], xa.at[dy, :, l2], side))
 
     cols = [slice(c, c + w) for c, w in STEPS]
     window = [pl.ds(c, w) for c, w in STEPS]
-    cot_in = local(cot, cn)
-    wgt_in = [local(wgt.at[:, c], wv.at[:, c]) for c in window]
-
-    row, lane = iota((576, 128), 0), iota((576, 128), 1)
-    which, slot = lax.div(row, 192), lax.div(lax.rem(row, 192), S1)
+    mine, theirs = pl.multiple_of(core * MINE, 128), pl.multiple_of((1 - core) * MINE, 128)
+    cot_in = [local(cot.at[:, :, pl.ds(first, MINE)], cn.at[h]) for h, first in enumerate((theirs, mine))]
+    wgt_in = [local(wgt.at[:, pl.ds(pl.multiple_of(mine + c, 128), w)], wv.at[:, pl.ds(c, w)]) for c, w in STEPS]
+
+    row, lane = iota((D, 128), 0), iota((D, 128), 1)
+    which, slot = lax.div(row, 8 * S1), lax.div(lax.rem(row, 8 * S1), S1)
     half, first = jnp.zeros_like(row), jnp.zeros_like(row)
     for p, (d, h) in enumerate(SLOTS):
         first = jnp.where(slot == p, d, first)
@@ -182,19 +182,19 @@
     second = half * 2 + lax.div(lax.rem(row, S1), S2)
     third = lax.div(lax.rem(row, S2), S3)
     at = {}
-    for axis, mine in (("x", x), ("y", y), ("z", z)):
+    for axis, place in (("x", x), ("y", y), ("z", z)):
         far = jnp.zeros_like(row)
         for s in range(3):
             far = jnp.where(which == s, (first, second, third)[ORDER[s].index(axis)], far)
-        at[axis] = lax.rem(far + mine, 4)
-    owner = (lax.div(at["x"], 2) * 2 + core) * 32 + at["z"] * 8 + at["y"] * 2 + lax.rem(at["x"], 2)
-    wanted = owner * 9 + which * S3 + lax.rem(row, S3)
+        at[axis] = lax.rem(far + place, 4)
+    keeper = jnp.where(lax.rem(row, S3) < 3, 0, 1)
+    owner = (lax.div(at["x"], 2) * 2 + keeper) * 32 + at["z"] * 8 + at["y"] * 2 + lax.rem(at["x"], 2)
+    wanted = owner * 9 + which * 3 + lax.rem(row, 3)
     for k in range(D // 128):
         sel[:, 128 * k : 128 * k + 128] = jnp.where(wanted == lane + 128 * k, 1.0, 0.0).astype(BF16)
 
     def take(dy):
-        for copy in x_first[dy]:
-            copy.wait_recv()
+        x_first[dy].wait_recv()
         xa[dy] = add16(xa[dy], part[dy, 0, :, 0:XL])
 
     take(2)
@@ -211,14 +211,20 @@
     take(3)
     near_down2 = [send(xa.at[3, :, l1], xnd.at[:, l1], down)]
 
-    cot_in.wait()
-
-    @pl.loop(0, 10)
-    def _(i):
-        cv[pl.ds(pl.multiple_of(i * 16, 16), 16), :] = cn[pl.ds(i * 8, 8)].reshape(16, H)
-
-    cot_tail = jnp.concatenate([cn[80].astype(F32), jnp.zeros((14, H), F32)], axis=0)
-    cv[160:176, :] = cot_tail.astype(BF16)
+    for h, dst in enumerate((cx, cv)):
+        cot_in[h].wait()
+
+        @pl.loop(0, 10)
+        def _(i):
+            dst[pl.ds(pl.multiple_of(i * 16, 16), 16), :] = cn[h, pl.ds(i * 8, 8)].reshape(16, MINE)
+
+        cot_tail = jnp.concatenate([cn[h, 80].astype(F32), jnp.zeros((14, MINE), F32)], axis=0)
+        dst[160:176, :] = cot_tail.astype(BF16)
+        if h == 0:
+            cot_twin = send(cx, cv.at[pl.ds(PADDED, PADDED)], twin)
+    for k in range(2):
+        gr[DEPTH * k + PADDED : DEPTH * k + DEPTH, :] = jnp.zeros((DEPTH - PADDED, MINE), BF16)
+    pt[:, 128:256] = jnp.zeros((D, 128), BF16)
 
     far_up2.wait_recv()
     xfu[...] = add16(xfu[...], xa[1, :, 0 : XL // 2])
@@ -254,7 +260,12 @@
     )
     pooled_twin = send(pb.at[pl.ds(0, PADDED)], pb.at[pl.ds(PADDED, PADDED)], twin)
 
-    grad_twin = []
+    pt[:, 0:PADDED] = lax.dot_general(
+        sel[...], pb[0:PADDED, :], (((1,), (1,)), ((), ())), preferred_element_type=F32
+    ).astype(BF16)
+    rows_twin = send(pt.at[:, pl.ds(0, DEPTH)], pt.at[:, pl.ds(DEPTH, DEPTH)], twin)
+
+    act_twin = []
 
     def gelu_rows(values, cotangent):
         square = values * values
@@ -264,25 +275,27 @@
         return (values * plus).astype(BF16), (cotangent * slope).astype(BF16)
 
     def product(j):
-        pre[j % 2, :, 0 : STEPS[j][1]] = jnp.dot(pb[0:PADDED, :], wv[:, cols[j]], preferred_element_type=F32)
+        pre[j % 2, :, 0 : STEPS[j][1]] = jnp.dot(pb[...], wv[:, cols[j]], preferred_element_type=F32)
 
     def forward(j):
-        for i in range(11):
+        for i in range(22):
             rows = slice(16 * i, 16 * i + 16)
+            base = 16 * i if i < 11 else 16 * i - PADDED + DEPTH
             act, grad = gelu_rows(pre[j % 2, rows, 0 : STEPS[j][1]], cv[rows, cols[j]].astype(F32))
             pa[rows, cols[j]] = act
-            gr[rows, cols[j]] = grad
-
-    def share(j):
-        grad_twin.append(
-            send(gr.at[pl.ds(0, PADDED), window[j]], gr.at[pl.ds(PADDED, PADDED), window[j]], twin)
-        )
-
-    def give(j):
+            gr[base : base + 16, cols[j]] = grad
+        act_twin.append(send(pa.at[pl.ds(PADDED, PADDED), window[j]], px.at[:, window[j]], twin))
+
+    def give(j, from_twin):
+        if from_twin:
+            act_twin[j].wait_recv()
+        c, w = STEPS[j]
+        source, first = (px, theirs) if from_twin else (pa, mine)
+        columns = pl.ds(pl.multiple_of(first + c, 128), w)
         for i in range(10):
-            rows = pa[16 * i : 16 * i + 16, cols[j]]
-            out_proj[8 * i : 8 * i + 8, :, cols[j]] = rows.reshape(8, 2, STEPS[j][1])
-        out_proj[80, :, cols[j]] = pa[160:162, cols[j]]
+            rows = source[16 * i : 16 * i + 16, cols[j]]
+            out_proj[8 * i : 8 * i + 8, :, columns] = rows.reshape(8, 2, w)
+        out_proj[80, :, columns] = source[160:162, cols[j]]
 
     msg = {}
 
@@ -294,11 +307,10 @@
         return a.astype(F32) + b.astype(F32) + c.astype(F32)
 
     def backward(j):
-        grad_twin[j].wait_recv()
         got = jnp.dot(pt[...], gr[:, cols[j]], preferred_element_type=F32)
         for s in range(3):
             for p in range(8):
-                base = s * 192 + p * S1
+                base = (s * 8 + p) * S1
                 g[s, p, :, cols[j]] = got[base : base + S1].astype(BF16)
         c = window[j]
         for s in range(3):
@@ -355,29 +367,37 @@
             total = r2[s, 0, :, c].astype(F32)
             for d in (1, 2, 3):
                 total = total + r3[s, d, :, c].astype(F32)
-            out_grad[S3 * s : S3 * s + S3, c] = total
-
-    settle()
+            own[s, :, c] = jnp.where(core == 0, total[0:3], total[3:6])
+            fin[s, :, c] = jnp.where(core == 0, total[3:6], total[0:3]).astype(BF16)
+        w = pl.ds(*GROUPS[q])
+        msg["swap", q] = send(fin.at[:, :, w], fin_twin.at[:, :, w], twin)
+
+    def swapped(q):
+        c = slice(GROUPS[q][0], sum(GROUPS[q]))
+        wait(("swap", q))
+        for s in range(3):
+            here_half, there_half = own[s, :, c], fin_twin[s, :, c].astype(F32)
+            rows = slice(3 * s, 3 * s + 3)
+            out_grad[rows, c] = jnp.where(core == 0, here_half, there_half)
+            out_grad[rows, slice(c.start + MINE, c.stop + MINE)] = jnp.where(core == 0, there_half, here_half)
+
     for copy in wgt_in:
         copy.wait()
-
-    def step(j):
-        product(j)
-        forward(j)
-        share(j)
-
-    step(0)
-    step(1)
+    cot_twin.wait_recv()
     pooled_twin.wait_recv()
-    pt[...] = lax.dot_general(
-        sel[...], pb[...], (((1,), (1,)), ((), ())), preferred_element_type=F32
-    ).astype(BF16)
+    product(0)
+    forward(0)
+    rows_twin.wait_recv()
     backward(0)
-    step(2)
+    product(1)
+    forward(1)
     backward(1)
-    step(3)
+    product(2)
+    forward(2)
     relay(0)
     backward(2)
+    product(3)
+    forward(3)
     relay(1)
     backward(3)
     relay(2)
@@ -386,17 +406,23 @@
     finish(1)
     finish(2)
     second_stage(0)
-    give(0)
+    give(0, False)
+    give(1, False)
     finish(3)
     second_stage(1)
-    give(1)
+    give(2, False)
+    give(3, False)
     third_stage(0)
-    give(2)
+    give(0, True)
+    give(1, True)
     settle()
     third_stage(1)
-    give(3)
     owned(0)
+    give(2, True)
     owned(1)
+    give(3, True)
+    swapped(0)
+    swapped(1)
     settle()
 
 
@@ -425,15 +451,16 @@
         in_specs=[any_spec] * 5,
         out_specs=(vmem_spec, vmem_spec),
         scratch_shapes=[
-            vm(D, H), vm(PADDED, H), vm(576, D),
-            vm(2, TOKS * POOL, D), vm(TOKS, 2, H), vm(256, 256), vm(4, 2, ROWS, D),
+            vm(D, MINE), vm(2 * PADDED, MINE), vm(PADDED, MINE), vm(D, D),
+            vm(2, TOKS * POOL, D), vm(2, TOKS, 2, MINE), vm(256, 256), vm(4, 2, ROWS, D),
             vm(4, ROWS, XL), vm(ROWS, XL // 2), vm(ROWS, XL // 2), vm(ROWS, XL), vm(ROWS, XL),
             vm(ROWS, YL), vm(ROWS, YL), vm(2, ROWS, YL), vm(2, ROWS, YL), vm(ROWS, YL), vm(ROWS, YL),
             pltpu.VMEM(shot_ids.shape, jnp.int32), pltpu.SMEM(band_width.shape, jnp.int32),
-            vm(PADDED, H), pltpu.VMEM((2, PADDED, WIDEST), F32),
-            vm(2 * PADDED, D), vm(576, 2 * PADDED), vm(2 * PADDED, H),
-            vm(3, 8, S1, H), vm(3, 2, S1, H), vm(3, 2, S1, H), vm(3, S1, H), vm(3, S1, H),
-            vm(3, 4, S2, H), vm(3, 4, S2, H), vm(3, 4, S3, H), vm(3, 4, S3, H),
+            vm(2 * PADDED, MINE), vm(PADDED, MINE), pltpu.VMEM((2, 2 * PADDED, WIDEST), F32),
+            vm(2 * PADDED, D), vm(D, 2 * DEPTH), vm(2 * DEPTH, MINE),
+            vm(3, 8, S1, MINE), vm(3, 2, S1, MINE), vm(3, 2, S1, MINE), vm(3, S1, MINE), vm(3, S1, MINE),
+            vm(3, 4, S2, MINE), vm(3, 4, S2, MINE), vm(3, 4, S3, MINE), vm(3, 4, S3, MINE),
+            pltpu.VMEM((3, 3, MINE), F32), vm(3, 3, MINE), vm(3, 3, MINE),
             sems(12), sems(128), sems(128),
         ],
         compiler_params=pltpu.CompilerParams(

time: 67.6 us -> 66.3 us (0.981)
  the two profiles are of different devices: /device:TPU:0 before, /device:TPU:1 now
where the time goes in v11:
time: 66.3 us; the launch traced here: 66.1 us
  Pallas kernels  65.3 us (98%)
  between operations  0.8 us (1%)
    pallas_call x1, Pallas kernels, per_device(): pl.pallas_call(kernel, out_shape=(pltpu.VMEM(cot.shape, BF16), pltpu.VMEM...  64.2 us

profile of v11, /device:TPU:1, one launch (start us, length us, event | category | flops | bytes accessed | tf_op | source)
XLA Modules:
  0.0 66.1 jit_solution(16694196445396303878)
XLA Ops:
  0.6 64.2 %shard_map.68 = (bf16[81,2,3584]{2,1,0:T(2,128)(2,1)S(1)}, f32[9,3584]{1,0:T(8,128)S(1)}) custom-call(bf16[2,648,1152]{2,1,0:T(8,128)(2,1)} %bitcast.9, bf16[1152,3584]{1,0:T(8,128)(2,1)} %wgt.1, bf16[81,2,3584]{2,1,0:T(2,128)(2,1)} %bitcast.10, s32[2,256]{1,0:T(2,128)} %shots_in.1, s32[2,4]{1,0:T(2,128)} %band_in.1), custom_call_target="tpu_custom_call" | custom-call | flops 4000000000 | bytes 14000000 | tf_op jit(solution)/shard_map/pallas_call | solution.py:448
  64.8 1.2 %shard_map.69 = (bf16[81,2,3584]{2,1,0:T(2,128)(2,1)}, f32[9,3584]{1,0:T(8,128)}) custom-call(bf16[81,2,3584]{2,1,0:T(2,128)(2,1)S(1)} %get-tuple-element.6.projected, f32[9,3584]{1,0:T(8,128)S(1)} %get-tuple-element.7.weight_grad), custom_call_target="tpu_custom_call" | custom-call | tf_op jit(solution)/shard_map/pallas_call | solution.py:473

commit v12 on v9

--- a/solution.py
+++ b/solution.py
@@ -331,16 +331,17 @@
                 for c in range(4):
                     r2[s, c, j] = value[S3 * c : S3 * c + S3].astype(BF16)
 
-    def third_stage():
+    def third_stage(q):
+        steps = pl.ds(2 * q, 2)
         for s in range(3):
             to = hop[ORDER[s][2]]
             for d in (2, 1, 3):
-                msg["last", s, d] = send(r2.at[s, d], r3.at[s, d], to[d])
-
-    def owned():
-        for s in range(3):
-            wait(*(("last", s, d) for d in (1, 2, 3)))
-            for j in range(4):
+                msg["last", s, q, d] = send(r2.at[s, d, steps], r3.at[s, d, steps], to[d])
+
+    def owned(q):
+        for s in range(3):
+            wait(*(("last", s, q, d) for d in (1, 2, 3)))
+            for j in (2 * q, 2 * q + 1):
                 total = r2[s, 0, j].astype(F32)
                 for d in (1, 2, 3):
                     total = total + r3[s, d, j].astype(F32)
@@ -369,23 +370,25 @@
     backward(2)
     relay(1)
     backward(3)
-    give(0)
     relay(2)
-    give(1)
     finish(0)
     finish(1)
     second_stage(0)
     relay(3)
-    give(2)
     finish(2)
+    give(0)
     finish(3)
     second_stage(1)
     second_finish(0)
+    third_stage(0)
+    give(1)
     settle()
     second_finish(1)
-    third_stage()
+    third_stage(1)
+    give(2)
+    owned(0)
     give(3)
-    owned()
+    owned(1)
     settle()
 
 
@@ -425,7 +428,7 @@
             vm(3, 4, 2, S1, CHUNK), vm(3, 4, 2, S1, CHUNK), vm(3, 4, S1, CHUNK), vm(3, 4, S1, CHUNK),
             vm(3, 4, 4, S2, CHUNK), vm(3, 4, 4, S2, CHUNK),
             vm(3, 4, 4, S3, CHUNK), vm(3, 4, 4, S3, CHUNK),
-            sems(12), sems(108), sems(108),
+            sems(12), sems(128), sems(128),
         ],
         compiler_params=pltpu.CompilerParams(
             collective_id=0, has_side_effects=True, vmem_limit_bytes=50 * 1024 * 1024

time: 65.5 us -> 65.4 us (level)
  no operation moved by 1% of the time
where the time goes in v12:
time: 65.4 us; the launch traced here: 65.3 us
  Pallas kernels  64.5 us (99%)
  between operations  0.8 us (1%)
    pallas_call x1, Pallas kernels, per_device(): pl.pallas_call(kernel, out_shape=(pltpu.VMEM(cot.shape, BF16), pltpu.VMEM...  63.3 us

profile of v12, /device:TPU:0, one launch (start us, length us, event | category | flops | bytes accessed | tf_op | source)
XLA Modules:
  0.0 65.3 jit_solution(4117649937307801047)
XLA Ops:
  0.6 63.3 %shard_map.68 = (bf16[81,2,3584]{2,1,0:T(2,128)(2,1)S(1)}, f32[9,3584]{1,0:T(8,128)S(1)}) custom-call(bf16[2,648,1152]{2,1,0:T(8,128)(2,1)} %bitcast.9, bf16[1152,3584]{1,0:T(8,128)(2,1)} %wgt.1, bf16[81,2,3584]{2,1,0:T(2,128)(2,1)} %bitcast.10, s32[2,256]{1,0:T(2,128)} %shots_in.1, s32[2,4]{1,0:T(2,128)} %band_in.1), custom_call_target="tpu_custom_call" | custom-call | flops 4000000000 | bytes 14000000 | tf_op jit(solution)/shard_map/pallas_call | solution.py:414
  64.0 1.2 %shard_map.69 = (bf16[81,2,3584]{2,1,0:T(2,128)(2,1)}, f32[9,3584]{1,0:T(8,128)}) custom-call(bf16[81,2,3584]{2,1,0:T(2,128)(2,1)S(1)} %get-tuple-element.6.projected, f32[9,3584]{1,0:T(8,128)S(1)} %get-tuple-element.7.weight_grad), custom_call_target="tpu_custom_call" | custom-call | tf_op jit(solution)/shard_map/pallas_call | solution.py:440

commit v13 on v12

--- a/solution.py
+++ b/solution.py
@@ -18,7 +18,7 @@
 YL = D - XL
 CHUNK = H // 4
 ORDER = (("z", "y", "x"), ("y", "x", "z"), ("x", "z", "y"))
-SLOTS = ((2, 0), (1, 1), (2, 1), (3, 0), (1, 0), (3, 1), (0, 0), (0, 1))
+SLOTS = tuple((d, h) for d in range(4) for h in range(2))
 S1, S2, S3 = 24, 12, 3
 C0 = 0.7978845608028654
 C1 = 0.044715
@@ -92,7 +92,7 @@
     xa, xfu, xfd, xnu, xnd, yfu, yfd, ynu, ynd, sb, yx,
     ids_v, band_s,
     pa, pre, pb, pt, gr, g,
-    ru, rd, nu, nd, r1, in2, r2, r3,
+    in1, r1, in2, r2, r3,
     local_sem, send_sem, recv_sem,
 ):
     here = Place(local_sem, send_sem, recv_sem)
@@ -293,27 +293,16 @@
             for p in range(8):
                 base = s * 192 + p * S1
                 g[s, j, p] = got[base : base + S1].astype(BF16)
-        for s in range(3):
-            to = hop[ORDER[s][0]]
-            msg["ru", s, j] = send(g.at[s, j, pl.ds(0, 2)], ru.at[s, j], to[1])
-            msg["rd", s, j] = send(g.at[s, j, pl.ds(2, 2)], rd.at[s, j], to[3])
-
-    def relay(j):
-        for s in range(3):
-            to = hop[ORDER[s][0]]
-            wait(("ru", s, j))
-            ru[s, j, 0] = add16(ru[s, j, 0], g[s, j, 4])
-            msg["nu", s, j] = send(ru.at[s, j, 0], nu.at[s, j], to[1])
-            wait(("rd", s, j))
-            rd[s, j, 0] = add16(rd[s, j, 0], g[s, j, 5])
-            msg["nd", s, j] = send(rd.at[s, j, 0], nd.at[s, j], to[3])
+        for d in (2, 1, 3):
+            for s in range(3):
+                to = hop[ORDER[s][0]][d]
+                msg["first", s, j, d] = send(g.at[s, j, pl.ds(2 * d, 2)], in1.at[s, j, d], to)
 
     def finish(j):
         for s in range(3):
-            wait(("nu", s, j), ("nd", s, j))
-            for h, value in enumerate(
-                (add3(g[s, j, 6], nu[s, j], rd[s, j, 1]), add3(g[s, j, 7], ru[s, j, 1], nd[s, j]))
-            ):
+            wait(*(("first", s, j, d) for d in (1, 2, 3)))
+            for h in range(2):
+                value = add3(g[s, j, h], in1[s, j, 1, h], in1[s, j, 3, h]) + in1[s, j, 2, h].astype(F32)
                 for b in range(2):
                     r1[s, 2 * h + b, j] = value[S2 * b : S2 * b + S2].astype(BF16)
 
@@ -366,15 +355,11 @@
     step(2)
     backward(1)
     step(3)
-    relay(0)
     backward(2)
-    relay(1)
     backward(3)
-    relay(2)
     finish(0)
     finish(1)
     second_stage(0)
-    relay(3)
     finish(2)
     give(0)
     finish(3)
@@ -425,7 +410,7 @@
             vm(4, PADDED, CHUNK), pltpu.VMEM((2, PADDED, CHUNK), F32),
             vm(2 * PADDED, D), vm(576, 2 * PADDED), vm(4, 2 * PADDED, CHUNK),
             vm(3, 4, 8, S1, CHUNK),
-            vm(3, 4, 2, S1, CHUNK), vm(3, 4, 2, S1, CHUNK), vm(3, 4, S1, CHUNK), vm(3, 4, S1, CHUNK),
+            vm(3, 4, 4, 2, S1, CHUNK),
             vm(3, 4, 4, S2, CHUNK), vm(3, 4, 4, S2, CHUNK),
             vm(3, 4, 4, S3, CHUNK), vm(3, 4, 4, S3, CHUNK),
             sems(12), sems(128), sems(128),

time: 65.4 us -> 66.4 us (1.015)
  Pallas kernels: 64.5 us -> 65.5 us
    pallas_call x1, Pallas kernels: 63.3 us -> 64.3 us  [per_device(): pl.pallas_call(kernel, out_shape=(pltpu.VMEM(cot.shape, BF16), pltpu.VMEM...]
where the time goes in v13:
time: 66.4 us; the launch traced here: 66.3 us
  Pallas kernels  65.5 us (99%)
  between operations  0.8 us (1%)
    pallas_call x1, Pallas kernels, per_device(): pl.pallas_call(kernel, out_shape=(pltpu.VMEM(cot.shape, BF16), pltpu.VMEM...  64.3 us

profile of v13, /device:TPU:0, one launch (start us, length us, event | category | flops | bytes accessed | tf_op | source)
XLA Modules:
  0.0 66.3 jit_solution(232879042375543771)
XLA Ops:
  0.6 64.3 %shard_map.68 = (bf16[81,2,3584]{2,1,0:T(2,128)(2,1)S(1)}, f32[9,3584]{1,0:T(8,128)S(1)}) custom-call(bf16[2,648,1152]{2,1,0:T(8,128)(2,1)} %bitcast.9, bf16[1152,3584]{1,0:T(8,128)(2,1)} %wgt.1, bf16[81,2,3584]{2,1,0:T(2,128)(2,1)} %bitcast.10, s32[2,256]{1,0:T(2,128)} %shots_in.1, s32[2,4]{1,0:T(2,128)} %band_in.1), custom_call_target="tpu_custom_call" | custom-call | flops 4000000000 | bytes 14000000 | tf_op jit(solution)/shard_map/pallas_call | solution.py:399
  65.0 1.2 %shard_map.69 = (bf16[81,2,3584]{2,1,0:T(2,128)(2,1)}, f32[9,3584]{1,0:T(8,128)}) custom-call(bf16[81,2,3584]{2,1,0:T(2,128)(2,1)S(1)} %get-tuple-element.6.projected, f32[9,3584]{1,0:T(8,128)S(1)} %get-tuple-element.7.weight_grad), custom_call_target="tpu_custom_call" | custom-call | tf_op jit(solution)/shard_map/pallas_call | solution.py:425

commit v14 on v12

--- a/solution.py
+++ b/solution.py
@@ -357,16 +357,16 @@
         share(j)
 
     step(0)
-    step(1)
     pooled_twin.wait_recv()
     pt[...] = lax.dot_general(
         sel[...], pb[...], (((1,), (1,)), ((), ())), preferred_element_type=F32
     ).astype(BF16)
     backward(0)
+    step(1)
     step(2)
     backward(1)
+    relay(0)
     step(3)
-    relay(0)
     backward(2)
     relay(1)
     backward(3)

time: 65.4 us -> 65.6 us (level)
  no operation moved by 1% of the time
where the time goes in v14:
time: 65.6 us; the launch traced here: 65.5 us
  Pallas kernels  64.7 us (99%)
  between operations  0.8 us (1%)
    pallas_call x1, Pallas kernels, per_device(): pl.pallas_call(kernel, out_shape=(pltpu.VMEM(cot.shape, BF16), pltpu.VMEM...  63.5 us

profile of v14, /device:TPU:0, one launch (start us, length us, event | category | flops | bytes accessed | tf_op | source)
XLA Modules:
  0.0 65.5 jit_solution(65041167438762034)
XLA Ops:
  0.6 63.5 %shard_map.68 = (bf16[81,2,3584]{2,1,0:T(2,128)(2,1)S(1)}, f32[9,3584]{1,0:T(8,128)S(1)}) custom-call(bf16[2,648,1152]{2,1,0:T(8,128)(2,1)} %bitcast.9, bf16[1152,3584]{1,0:T(8,128)(2,1)} %wgt.1, bf16[81,2,3584]{2,1,0:T(2,128)(2,1)} %bitcast.10, s32[2,256]{1,0:T(2,128)} %shots_in.1, s32[2,4]{1,0:T(2,128)} %band_in.1), custom_call_target="tpu_custom_call" | custom-call | flops 4000000000 | bytes 14000000 | tf_op jit(solution)/shard_map/pallas_call | solution.py:414
  64.1 1.2 %shard_map.69 = (bf16[81,2,3584]{2,1,0:T(2,128)(2,1)}, f32[9,3584]{1,0:T(8,128)}) custom-call(bf16[81,2,3584]{2,1,0:T(2,128)(2,1)S(1)} %get-tuple-element.6.projected, f32[9,3584]{1,0:T(8,128)S(1)} %get-tuple-element.7.weight_grad), custom_call_target="tpu_custom_call" | custom-call | tf_op jit(solution)/shard_map/pallas_call | solution.py:440

commit v15 on v12

--- a/solution.py
+++ b/solution.py
@@ -101,8 +101,8 @@
     la, lb = pl.ds(0, XL), pl.ds(XL, YL)
     ids_in = local(shots_in, ids_v)
     width_in = local(band_in, band_s)
+    feat_b = local(feat.at[:, :, lb], fv.at[:, :, lb])
     feat_a = local(feat.at[:, :, la], fv.at[:, :, la])
-    feat_b = local(feat.at[:, :, lb], fv.at[:, :, lb])
 
     everybody = here.greet([hop[a][d] for a in "xyz" for d in (1, 2, 3)] + [twin])
 
@@ -152,16 +152,16 @@
     l1, l2 = pl.ds(0, XL // 2), pl.ds(XL // 2, XL // 2)
     up, down, side = hop["y"][1], hop["y"][3], here.mate
 
-    feat_a.wait()
-    partial_sums(slice(0, XL))
-    everybody()
-    x_first = {dy: send(part.at[dy, 1, :, la], xa.at[dy], side) for dy in (2, 1, 3, 0)}
     feat_b.wait()
     partial_sums(slice(XL, D))
+    everybody()
     far_up = send(part.at[2, 0, :, lb], yfu, up)
     far_down = send(part.at[2, 1, :, lb], yfd, down)
     near_up = {1: send(part.at[1, 1, :, lb], ynu.at[1], up)}
     near_down = {0: send(part.at[3, 0, :, lb], ynd.at[0], down)}
+    feat_a.wait()
+    partial_sums(slice(0, XL))
+    x_first = {dy: send(part.at[dy, 1, :, la], xa.at[dy], side) for dy in (2, 1, 3, 0)}
 
     columns = [pl.ds(j * CHUNK, CHUNK) for j in range(4)]
     cot_in = [local(cot.at[:, :, columns[j]], cn.at[j]) for j in range(4)]
@@ -190,14 +190,14 @@
         x_first[dy].wait_recv()
         xa[dy] = add16(xa[dy], part[dy, 0, :, 0:XL])
 
-    take(2)
-    far_up2 = send(xa.at[2, :, l1], xfu, up)
     far_up.wait_recv()
     yfu[...] = add16(yfu[...], part[1, 0, :, XL:D])
     near_up[0] = send(yfu, ynu.at[0], up)
     far_down.wait_recv()
     yfd[...] = add16(yfd[...], part[3, 1, :, XL:D])
     near_down[1] = send(yfd, ynd.at[1], down)
+    take(2)
+    far_up2 = send(xa.at[2, :, l1], xfu, up)
     far_down2 = send(xa.at[2, :, l2], xfd, down)
     take(1)
     near_up2 = [send(xa.at[1, :, l2], xnu.at[:, l2], up)]

time: 65.4 us -> 66.1 us (1.011)
  Pallas kernels: 64.5 us -> 65.2 us
    pallas_call x1, Pallas kernels: 63.3 us -> 64 us  [per_device(): pl.pallas_call(kernel, out_shape=(pltpu.VMEM(cot.shape, BF16), pltpu.VMEM...]
where the time goes in v15:
time: 66.1 us; the launch traced here: 66 us
  Pallas kernels  65.2 us (99%)
  between operations  0.8 us (1%)
    pallas_call x1, Pallas kernels, per_device(): pl.pallas_call(kernel, out_shape=(pltpu.VMEM(cot.shape, BF16), pltpu.VMEM...  64 us

profile of v15, /device:TPU:0, one launch (start us, length us, event | category | flops | bytes accessed | tf_op | source)
XLA Modules:
  0.0 66.0 jit_solution(1695701041959682214)
XLA Ops:
  0.6 64.0 %shard_map.68 = (bf16[81,2,3584]{2,1,0:T(2,128)(2,1)S(1)}, f32[9,3584]{1,0:T(8,128)S(1)}) custom-call(bf16[2,648,1152]{2,1,0:T(8,128)(2,1)} %bitcast.9, bf16[1152,3584]{1,0:T(8,128)(2,1)} %wgt.1, bf16[81,2,3584]{2,1,0:T(2,128)(2,1)} %bitcast.10, s32[2,256]{1,0:T(2,128)} %shots_in.1, s32[2,4]{1,0:T(2,128)} %band_in.1), custom_call_target="tpu_custom_call" | custom-call | flops 4000000000 | bytes 14000000 | tf_op jit(solution)/shard_map/pallas_call | solution.py:414
  64.7 1.2 %shard_map.69 = (bf16[81,2,3584]{2,1,0:T(2,128)(2,1)}, f32[9,3584]{1,0:T(8,128)}) custom-call(bf16[81,2,3584]{2,1,0:T(2,128)(2,1)S(1)} %get-tuple-element.6.projected, f32[9,3584]{1,0:T(8,128)S(1)} %get-tuple-element.7.weight_grad), custom_call_target="tpu_custom_call" | custom-call | tf_op jit(solution)/shard_map/pallas_call | solution.py:440
